TPU v7x, 32 devices: a whole 2x2x4 slice. The times are simulated.
32 devices in a mesh: wide: 8 (over z, x), narrow: 4 (over y, core).
Axes of the slice: x: 2, y: 2, z: 4, core: 2. Of those that a mesh axis runs over, the one named last changes fastest.
Arguments:
- layer_argument: bfloat16 [20480, 768], P('wide'), may hold values from -6 to 6
- document_extents: int32 [8, 4], P('wide'), may hold values from 1 to 1024, as said below
- distance_bin_lookup: int32 [2047], replicated, may hold values from 0 to 31, as said below
- tile_location: int32 [13], replicated, may hold values from 0 to 15, as said below
- precise_parameter_blocks: float32 [16, 768, 768], P('wide', 'narrow'), may hold values from -0.21875 to 0.21875
- precise_mean_est: float32 [16, 768, 768], P('wide', 'narrow'), may hold values from -2.2888184e-05 to 2.2888184e-05
- precise_variance_est: float32 [16, 768, 768], P('wide', 'narrow'), may hold values from 1.30417e-11 to 5.21668e-11
- rescaling_coefficients: float32 [3, 768], replicated, may hold values from 0.5 to 1.5
- norm_scale_mean_est: float32 [3, 768], replicated, may hold values from -9.1552734e-05 to 9.1552734e-05
- norm_scale_variance_est: float32 [3, 768], replicated, may hold values from 2.086672e-10 to 8.346688e-10
- distance_bias_table: float32 [32, 12], P(None, 'narrow'), may hold values from -6 to 6
- offset_bias_mean_est: float32 [32, 12], P(None, 'narrow'), may hold values from -3.0517578e-05 to 3.0517578e-05
- offset_bias_variance_est: float32 [32, 12], P(None, 'narrow'), may hold values from 1.30417e-11 to 5.21668e-11
- sharpness_exponent: float32 [1], replicated, may hold values from 3 to 3.7
- sharpness_mean_est: float32 [1], replicated, may hold values from -0.03125 to 0.03125
- sharpness_variance_est: float32 [1], replicated, may hold values from 2.5e-05 to 0.0001
Outputs:
- loss: float32 [], replicated
- layer_result: float32 [20480, 768], P('wide')
- input_grad: float32 [20480, 768], P('wide')
- grad_norm: float32 [], replicated
- slot_first: float32 [16, 768, 768], P('wide', 'narrow')
- slot_second: float32 [16, 768, 768], P('wide', 'narrow')
- slot_weight: float32 [16, 768, 768], P('wide', 'narrow')
- gain_first: float32 [3, 768], replicated
- gain_second: float32 [3, 768], replicated
- gain_new: float32 [3, 768], replicated
- bias_first: float32 [32, 12], P(None, 'narrow')
- bias_second: float32 [32, 12], P(None, 'narrow')
- bias_new: float32 [32, 12], P(None, 'narrow')
- sharpness_mean_fresh: float32 [1], replicated
- sharpness_variance_fresh: float32 [1], replicated
- sharpness_exponent_fresh: float32 [1], replicated
Inputs may be any that keep to these rules, and one draw needn't show every extreme that they name: `distance_bin_lookup`: bucket of a relative offset: offsets of size under 32 // 4 have their own buckets, larger ones share buckets that never fall with the offset's size; offsets above zero have 32 // 2 added. Distinct slots; block u belongs to index tile_location[u] // 2 of wide; some index of wide owns 2 blocks. `document_extents`: the lengths of a row add up to 2560.
All inputs are finite; a program needn't handle non-finite values.
Results may differ from a plain program's by a relative error of at most 0.03.
Values may be sent and summed in bfloat16 or wider, within the bound.
No kernel may reach another device: no remote copies, remote signals or barrier semaphores. Data moves between devices by JAX's collectives and lax.ppermute only.
A program may use at most 320 MiB of HBM per device.

v0:
```python
import jax
import jax.numpy as jnp
from jax import lax
from jax.experimental import pallas as pl
from jax.experimental.pallas import tpu as pltpu
from jax.sharding import Mesh
from jax.sharding import PartitionSpec as P

D = 768
FF = 3072
BUCKETS = 32
TOK_DEV = 2560
SEQS_DEV = 4
DOCLEN = 1024
CAP = 2
STEP = 10
LANE = 128
BQ = 512
BK = 512
UNIT_BLOCK = 768
REACH = DOCLEN // LANE
OFF = REACH + (BQ + BK) // LANE
SPAN = 2 * OFF + 1
LINES = 2 * REACH + 2
VMEM_LIMIT = 56 * 1024 * 1024

norm_eps = 1e-06
clip_limit = 0.01
learn_rate = 0.01
side_rate = 0.5
beta_one = 0.5
beta_two = 0.5
adam_eps = 1e-08
decay_rate = 0.01
score_scale = 0.125
masked_score = -1e30
low_type = jnp.bfloat16


def times_transposed(left_side, right_side):
    return lax.dot_general(
        left_side, right_side, (((1,), (1,)), ((), ())), preferred_element_type=jnp.float32
    )


def plain_product(left_side, right_side):
    return jnp.dot(left_side, right_side, preferred_element_type=jnp.float32)


def outer_product(left_side, right_side):
    return lax.dot_general(
        left_side, right_side, (((0,), (0,)), ((), ())), preferred_element_type=jnp.float32
    )


def rms_scale(values):
    return lax.rsqrt(jnp.mean(values * values, axis=-1, keepdims=True) + norm_eps)


def norm_backward(values, row_scale, gain_row, grad_out):
    weighted = grad_out * gain_row
    gain_grad = jnp.sum(grad_out * values * row_scale, axis=0)
    inner_mean = jnp.mean(weighted * values, axis=-1, keepdims=True)
    value_grad = row_scale * weighted - values * row_scale * row_scale * row_scale * inner_mean
    return (value_grad, gain_grad)


def decoupled_decay_step(gradient, first_moment, second_moment, weight, multiplier, step_rate):
    clipped = gradient * multiplier
    first_new = beta_one * first_moment + (1.0 - beta_one) * clipped
    second_new = beta_two * second_moment + (1.0 - beta_two) * clipped * clipped
    first_hat = first_new / (1.0 - beta_one**STEP)
    second_hat = second_new / (1.0 - beta_two**STEP)
    weight_new = weight - step_rate * (
        first_hat / (jnp.sqrt(second_hat) + adam_eps) + decay_rate * weight
    )
    return (first_new, second_new, weight_new)


def swap(values, axes, bit):
    count = lax.axis_size(axes)
    return lax.ppermute(values, axes, [(i, i ^ bit) for i in range(count)])


def sum_low(left, right):
    return (left.astype(jnp.float32) + right.astype(jnp.float32)).astype(low_type)


def narrow_bits(count):
    return [1 << s for s in range(count.bit_length() - 1)]


def peer_order(count):
    order = [0]
    for bit in reversed(narrow_bits(count)):
        order = order + [peer ^ bit for peer in order]
    return order


def join_rows(values, axes):
    for bit in reversed(narrow_bits(lax.axis_size(axes))):
        values = jnp.concatenate([values, swap(values, axes, bit)], axis=0)
    return values


def add_rows(values, axes):
    for bit in narrow_bits(lax.axis_size(axes)):
        half = values.shape[0] // 2
        came = swap(values[half:].astype(low_type), axes, bit)
        values = values[:half].astype(jnp.float32) + came.astype(jnp.float32)
    return values


def product_add_rows(left_side, right_side, axes):
    bits = narrow_bits(lax.axis_size(axes))
    half = left_side.shape[0] // 2
    sent = plain_product(left_side[half:], right_side).astype(low_type)
    came = swap(sent, axes, bits[0])
    values = plain_product(left_side[:half], right_side) + came.astype(jnp.float32)
    for bit in bits[1:]:
        half = values.shape[0] // 2
        came = swap(values[half:].astype(low_type), axes, bit)
        values = values[:half] + came.astype(jnp.float32)
    return values


def natural_rows(joined, places):
    group = joined.shape[0] // len(places)
    return jnp.concatenate(
        [lax.dynamic_slice_in_dim(joined, place * group, group, 0) for place in places], axis=0
    )


def spread(values, axes):
    copies = jnp.broadcast_to(values[None], (lax.axis_size(axes),) + values.shape)
    return lax.all_to_all(copies, axes, split_axis=0, concat_axis=0, tiled=True)


def after(values, other):
    return lax.optimization_barrier((values, other))[0]


def gelu_and_slope(values):
    rate = 0.7978845608028654
    cubic = 0.044715
    squares = values * values
    turn = jnp.tanh(rate * values * (1.0 + cubic * squares))
    half = 0.5 * (1.0 + turn)
    slope = half + 0.5 * values * (1.0 - turn * turn) * (rate * (1.0 + 3.0 * cubic * squares))
    return (values * half).astype(low_type), slope.astype(low_type)


def smem():
    return pl.BlockSpec(memory_space=pltpu.SMEM)


def vmem():
    return pl.BlockSpec(memory_space=pltpu.VMEM)


def bias_kernel(chunks, tiles):
    heads = tiles.shape[0]
    tiles[...] = jnp.zeros_like(tiles)
    for h in range(heads):
        for d in range(-REACH, REACH + 1):
            left = chunks[h, REACH + 1 - d : REACH + 2 - d, :]
            right = chunks[h, REACH - d : REACH + 1 - d, :]
            line = jnp.broadcast_to(jnp.concatenate([left, right], axis=1), (LANE, 2 * LANE))
            rolled = pltpu.roll(line, 0, 1, stride=1, stride_axis=0)
            tiles[h, (d + OFF) * LANE : (d + OFF + 1) * LANE, :] = rolled[:, :LANE]


def bias_tiles(rel_chunks):
    heads = rel_chunks.shape[0]
    return pl.pallas_call(
        bias_kernel,
        out_shape=jax.ShapeDtypeStruct((heads, SPAN * LANE, LANE), jnp.float32),
        compiler_params=pltpu.CompilerParams(vmem_limit_bytes=VMEM_LIMIT),
        name="bias_tiles",
    )(rel_chunks)


def key_range(lengths, first, last):
    start = jnp.int32(0)
    low = jnp.int32(0)
    high = jnp.int32(0)
    for s in range(SEQS_DEV):
        end = start + lengths[s]
        low = jnp.where(start <= first, start, low)
        high = jnp.where(start <= last, end, high)
        start = end
    return low // BK, (high + BK - 1) // BK


def bias_part(bias, h, row):
    return jnp.concatenate(
        [
            bias[h, pl.ds(pl.multiple_of(row - b * LANE, LANE), BK), :]
            for b in range(BQ // LANE)
        ],
        axis=1,
    )


def forward_kernel(first_row, lengths, origin, qT, kn, vT, apart, bias, ctx_o, ctxT_o, lse_o, qa, acc):
    width, rows_here = qT.shape
    heads = bias.shape[0]
    size = width // heads
    qa[...] = jnp.zeros_like(qa)

    @pl.loop(0, rows_here // BQ)
    def _(i):
        q0 = pl.multiple_of(i * BQ, BQ)
        here = pl.ds(q0, BQ)
        for h in range(heads):
            qa[h * LANE : h * LANE + size, :] = qT[h * size : (h + 1) * size, here]
            qa[h * LANE + size : h * LANE + size + 16, :] = apart[:, here]
        acc[...] = jnp.zeros_like(acc)
        low, high = key_range(lengths, first_row + q0, first_row + q0 + BQ - 1)

        def step(j, carry):
            k0 = pl.multiple_of(j * BK, BK)
            row = (j * (BK // LANE) - i * (BQ // LANE) - first_row // LANE + OFF) * LANE
            out = []
            for h in range(heads):
                top, total = carry[2 * h], carry[2 * h + 1]
                own = slice(h * LANE, (h + 1) * LANE)
                rows = slice(h * size, (h + 1) * size)
                s = plain_product(kn[pl.ds(k0, BK), own], qa[own, :]) + bias_part(bias, h, row)
                new_top = jnp.maximum(top, jnp.max(s, axis=0, keepdims=True))
                fade = jnp.exp(top - new_top)
                p = jnp.exp(s - new_top)
                total = total * fade + jnp.sum(p, axis=0, keepdims=True)
                acc[rows, :] = acc[rows, :] * fade + plain_product(
                    vT[rows, pl.ds(k0, BK)], p.astype(low_type)
                )
                out += [new_top, total]
            return tuple(out)

        init = tuple(
            jnp.full((1, BQ), 2.0 * masked_score if n % 2 == 0 else 0.0, jnp.float32)
            for n in range(2 * heads)
        )
        done = lax.fori_loop(low, high, step, init)
        for h in range(heads):
            rows = slice(h * size, (h + 1) * size)
            acc[rows, :] = acc[rows, :] / done[2 * h + 1]
            lse_o[h : h + 1, here] = done[2 * h] + jnp.log(done[2 * h + 1])
        ctxT_o[:, here] = acc[...]
        turned = acc[...].T.astype(low_type)
        for b in range(BQ // LANE):
            at = pl.multiple_of(origin[i * (BQ // LANE) + b], LANE)
            ctx_o[pl.ds(at, LANE), :] = turned[b * LANE : (b + 1) * LANE, :]


def attention_forward(first_row, lengths, origin, qT, kn, vT, apart, bias):
    width, rows_here = qT.shape
    heads = bias.shape[0]

    def body(*refs):
        forward_kernel(first_row, *refs)

    return pl.pallas_call(
        body,
        out_shape=(
            jax.ShapeDtypeStruct((rows_here, width), low_type),
            jax.ShapeDtypeStruct((width, rows_here), jnp.float32),
            jax.ShapeDtypeStruct((heads, rows_here), jnp.float32),
        ),
        in_specs=[smem()] * 2 + [vmem()] * 5,
        out_specs=(vmem(),) * 3,
        scratch_shapes=[
            pltpu.VMEM((heads * LANE, BQ), low_type),
            pltpu.VMEM((width, BQ), jnp.float32),
        ],
        compiler_params=pltpu.CompilerParams(vmem_limit_bytes=VMEM_LIMIT),
        cost_estimate=pl.CostEstimate(
            flops=rows_here * width, bytes_accessed=width * TOK_DEV, transcendentals=0
        ),
        name="attention_forward",
    )(lengths, origin, qT, kn, vT, apart, bias)


def three_parts(values):
    first = values.astype(low_type).astype(jnp.float32)
    rest = values - first
    second = rest.astype(low_type).astype(jnp.float32)
    return first, second, rest - second


def backward_kernel(
    lengths, origin, qT, kn, vn, kT, dcn, ctxT, lse, apart, bias,
    dT_o, dn_o, lines_o, qa, da, dq, dk, dv, tiles,
):
    width, tokens = qT.shape
    heads = bias.shape[0]
    size = width // heads
    for ref in (qa, da, dk, dv, tiles):
        ref[...] = jnp.zeros_like(ref)
    place = lax.broadcasted_iota(jnp.int32, (16, BQ), 0) - SEQS_DEV

    def in_depth(values):
        a, b, c = three_parts(values)
        return jnp.where(place == 0, a, jnp.where(place == 1, b, jnp.where(place == 2, c, 0.0)))

    @pl.loop(0, tokens // BQ)
    def _(i):
        q0 = pl.multiple_of(i * BQ, BQ)
        here = pl.ds(q0, BQ)
        at = [pl.multiple_of(origin[i * (BQ // LANE) + b], LANE) for b in range(BQ // LANE)]
        dcT = jnp.concatenate(
            [dcn[pl.ds(at[b], LANE), :].astype(jnp.float32) for b in range(BQ // LANE)], axis=0
        ).T
        for h in range(heads):
            rows = slice(h * size, (h + 1) * size)
            top = h * LANE
            qa[top : top + size, :] = qT[rows, here]
            extra = apart[:, here].astype(jnp.float32) + in_depth(-lse[h : h + 1, here])
            qa[top + size : top + size + 16, :] = extra.astype(low_type)
            da[top : top + size, :] = dcT[rows, :].astype(low_type)
            delta = jnp.sum(dcT[rows, :] * ctxT[rows, here], axis=0, keepdims=True)
            da[top + size : top + size + 16, :] = in_depth(-delta).astype(low_type)
        dq[...] = jnp.zeros_like(dq)
        low, high = key_range(lengths, q0, q0 + BQ - 1)

        @pl.loop(low, high)
        def _(j):
            k0 = pl.multiple_of(j * BK, BK)
            there = pl.ds(k0, BK)
            row = (j * (BK // LANE) - i * (BQ // LANE) + OFF) * LANE
            for h in range(heads):
                rows = slice(h * size, (h + 1) * size)
                own = slice(h * LANE, (h + 1) * LANE)
                flat = slice(h * LANE, h * LANE + size)
                s = plain_product(kn[there, own], qa[own, :])
                p = jnp.exp(s + bias_part(bias, h, row))
                ds = p * plain_product(vn[there, own], da[own, :])
                for b in range(BQ // LANE):
                    window = pl.ds(pl.multiple_of(row - b * LANE, LANE), BK)
                    tiles[h, window, :] = (
                        tiles[h, window, :] + ds[:, b * LANE : (b + 1) * LANE]
                    )
                p_low = p.astype(low_type)
                ds_low = ds.astype(low_type)
                dv[rows, there] = dv[rows, there] + times_transposed(da[flat, :], p_low)
                dk[rows, there] = dk[rows, there] + times_transposed(qa[flat, :], ds_low)
                dq[rows, :] = dq[rows, :] + plain_product(kT[rows, there], ds_low)

        grad = dq[...] * score_scale
        dT_o[0:width, here] = grad.astype(low_type)
        turned = grad.T.astype(low_type)
        for b in range(BQ // LANE):
            dn_o[pl.ds(at[b], LANE), 0:width] = turned[b * LANE : (b + 1) * LANE, :]

    @pl.loop(0, tokens // BQ)
    def _(i):
        here = pl.ds(pl.multiple_of(i * BQ, BQ), BQ)
        both = jnp.concatenate([dk[:, here], dv[:, here]], axis=0)
        dT_o[width : 3 * width, here] = both.astype(low_type)
        turned = both.T.astype(low_type)
        for b in range(BQ // LANE):
            at = pl.multiple_of(origin[i * (BQ // LANE) + b], LANE)
            dn_o[pl.ds(at, LANE), width : 3 * width] = turned[b * LANE : (b + 1) * LANE, :]

    across = lax.broadcasted_iota(jnp.int32, (LANE, LANE), 1)
    over = across >= lax.broadcasted_iota(jnp.int32, (LANE, LANE), 0)
    sub = lax.broadcasted_iota(jnp.int32, (8, LANE), 0)
    for h in range(heads):
        for d in range(-REACH, REACH + 2):
            here = tiles[h, (d + OFF) * LANE : (d + OFF + 1) * LANE, :]
            below = tiles[h, (d + OFF - 1) * LANE : (d + OFF) * LANE, :]
            mixed = jnp.where(over, here, below)
            line = mixed[LANE - 8 :, :]
            for g in range(LANE // 8 - 2, -1, -1):
                line = mixed[8 * g : 8 * g + 8, :] + pltpu.roll(line, LANE - 8, 1)
            for bit in (1, 2, 4):
                line = jnp.where((sub & bit) != 0, pltpu.roll(line, LANE - bit, 1), line)
            lines_o[h, REACH + 1 - d : REACH + 2 - d, :] = jnp.sum(line, axis=0, keepdims=True)


def attention_backward(lengths, origin, qT, kn, vn, kT, dcn, ctxT, lse, apart, bias):
    width, tokens = qT.shape
    heads = bias.shape[0]
    return pl.pallas_call(
        backward_kernel,
        out_shape=(
            jax.ShapeDtypeStruct((3 * width, tokens), low_type),
            jax.ShapeDtypeStruct((tokens, 3 * width), low_type),
            jax.ShapeDtypeStruct((heads, LINES, LANE), jnp.float32),
        ),
        in_specs=[smem()] * 2 + [vmem()] * 9,
        out_specs=(vmem(),) * 3,
        scratch_shapes=[
            pltpu.VMEM((heads * LANE, BQ), low_type),
            pltpu.VMEM((heads * LANE, BQ), low_type),
            pltpu.VMEM((width, BQ), jnp.float32),
            pltpu.VMEM((width, tokens), jnp.float32),
            pltpu.VMEM((width, tokens), jnp.float32),
            pltpu.VMEM((heads, SPAN * LANE, LANE), jnp.float32),
        ],
        compiler_params=pltpu.CompilerParams(vmem_limit_bytes=VMEM_LIMIT),
        cost_estimate=pl.CostEstimate(
            flops=tokens * width, bytes_accessed=width * TOK_DEV, transcendentals=0
        ),
        name="attention_backward",
    )(lengths, origin, qT, kn, vn, kT, dcn, ctxT, lse, apart, bias)


def feed_forward_backward_kernel(
    grad, rows, hidden, slope, inner, outer, weight_grads, rows_grad
):
    groups, _, size, width = weight_grads.shape

    @pl.when(pl.program_id(0) == 0)
    def _():
        rows_grad[...] = jnp.zeros_like(rows_grad)

    outer_grad = outer_product(hidden[...], grad[...]).astype(low_type)
    weight_grads[:, 0] = outer_grad.reshape(groups, size, width)
    pre = (
        times_transposed(grad[...], outer[...]) * slope[...].astype(jnp.float32)
    ).astype(low_type)
    inner_grad = outer_product(pre, rows[...]).astype(low_type)
    weight_grads[:, 1] = inner_grad.reshape(groups, size, width)
    rows_grad[...] += plain_product(pre, inner[...])


def feed_forward_backward(grad, rows, hidden, slope, inner, outer, size):
    count = grad.shape[0]
    groups = UNIT_BLOCK // size
    every = pl.BlockSpec((count, D), lambda i: (0, 0))
    units = pl.BlockSpec((count, UNIT_BLOCK), lambda i: (0, i))
    weight = pl.BlockSpec((UNIT_BLOCK, D), lambda i: (i, 0))
    return pl.pallas_call(
        feed_forward_backward_kernel,
        grid=(FF // UNIT_BLOCK,),
        out_shape=(
            jax.ShapeDtypeStruct((FF // size, 2, size, D), low_type),
            jax.ShapeDtypeStruct((count, D), jnp.float32),
        ),
        in_specs=[every, every, units, units, weight, weight],
        out_specs=(pl.BlockSpec((groups, 2, size, D), lambda i: (i, 0, 0, 0)), every),
        compiler_params=pltpu.CompilerParams(vmem_limit_bytes=VMEM_LIMIT),
        cost_estimate=pl.CostEstimate(flops=FF * D, bytes_accessed=FF * D, transcendentals=0),
        name="feed_forward_backward",
    )(grad, rows, hidden, slope, inner, outer)


def loss_kernel(place, numbers, parts, proj_weight, gain, out_slope, out_low, out_row, out_gain):
    total_seqs = out_low.shape[0] // 2
    terms = parts.shape[0] // total_seqs
    exact = dict(precision=lax.Precision.HIGHEST, preferred_element_type=jnp.float32)
    seq = lax.broadcasted_iota(jnp.int32, (total_seqs, parts.shape[0]), 0)
    part = lax.broadcasted_iota(jnp.int32, (total_seqs, parts.shape[0]), 1)
    joins = jnp.logical_and(
        seq // SEQS_DEV == part // (SEQS_DEV * terms), seq % SEQS_DEV == part % SEQS_DEV
    )
    unscaled = jnp.dot(joins.astype(jnp.float32), parts[...], **exact)
    pooled_low = (unscaled * gain[...]).astype(low_type)
    projected = times_transposed(pooled_low, proj_weight[...]).astype(low_type).astype(jnp.float32)
    inverse = lax.rsqrt(jnp.sum(projected * projected, axis=1, keepdims=True) + norm_eps)
    embed_low = (projected * inverse).astype(low_type)
    sharpness_factor = jnp.exp(jnp.full((1, 1), numbers[0], jnp.float32))
    agreement = times_transposed(embed_low, embed_low)
    row = lax.broadcasted_iota(jnp.int32, (total_seqs, total_seqs), 0)
    column = lax.broadcasted_iota(jnp.int32, (total_seqs, total_seqs), 1)
    logits = jnp.where(row == column, masked_score, sharpness_factor * agreement)
    partner = (row ^ 1) == column

    def log_sum(axis):
        top = jnp.max(logits, axis=axis, keepdims=True)
        return top + jnp.log(jnp.sum(jnp.exp(logits - top), axis=axis, keepdims=True))

    log_rows = log_sum(1)
    positive = jnp.where(partner, 1.0, 0.0)
    slope = (jnp.exp(logits - log_rows) - positive) / total_seqs
    slope_turned = (jnp.exp(logits - log_sum(0)) - positive) / total_seqs
    embed_grad = sharpness_factor * jnp.dot(
        slope + slope_turned, embed_low.astype(jnp.float32), **exact
    )
    along = jnp.sum(projected * embed_grad, axis=1, keepdims=True)
    proj_grad_low = (
        inverse * embed_grad - projected * inverse * inverse * inverse * along
    ).astype(low_type)
    pooled_grad = plain_product(proj_grad_low, proj_weight[...])
    out_low[0:total_seqs, :] = proj_grad_low
    out_low[total_seqs : 2 * total_seqs, :] = pooled_low
    out_gain[...] = jnp.sum(pooled_grad * unscaled, axis=0, keepdims=True)
    loss = jnp.sum(
        log_rows - jnp.sum(positive * jnp.where(partner, logits, 0.0), axis=1, keepdims=True),
        axis=0,
        keepdims=True,
    ) / total_seqs
    temperature = sharpness_factor * jnp.sum(
        jnp.sum(slope * agreement, axis=1, keepdims=True), axis=0, keepdims=True
    )
    lane = lax.broadcasted_iota(jnp.int32, (1, LANE), 1)
    out_row[...] = jnp.where(lane == 0, loss, jnp.where(lane == 1, temperature, 0.0))
    mine = lax.broadcasted_iota(jnp.int32, (8, total_seqs), 0)
    seq_of = lax.broadcasted_iota(jnp.int32, (8, total_seqs), 1) - place[0] * SEQS_DEV
    picks = jnp.logical_and(mine == seq_of, mine < SEQS_DEV).astype(jnp.float32)
    own = jnp.dot(picks, pooled_grad, **exact)
    index = lax.broadcasted_iota(jnp.int32, (8, 1), 0)
    extent = jnp.ones((8, 1), jnp.float32)
    for s in range(SEQS_DEV):
        extent = jnp.where(index == s, place[1 + s].astype(jnp.float32), extent)
    out_slope[...] = own * gain[...] / extent


def contrastive(place, numbers, parts, proj_weight, gain, total_seqs):
    return pl.pallas_call(
        loss_kernel,
        out_shape=(
            jax.ShapeDtypeStruct((8, D), jnp.float32),
            jax.ShapeDtypeStruct((2 * total_seqs, D), low_type),
            jax.ShapeDtypeStruct((1, LANE), jnp.float32),
            jax.ShapeDtypeStruct((1, D), jnp.float32),
        ),
        in_specs=[smem()] * 2 + [vmem()] * 3,
        out_specs=(vmem(),) * 4,
        compiler_params=pltpu.CompilerParams(vmem_limit_bytes=VMEM_LIMIT),
        cost_estimate=pl.CostEstimate(
            flops=4 * total_seqs * D * D, bytes_accessed=4 * D * D, transcendentals=total_seqs
        ),
        name="contrastive",
    )(place, numbers, parts, proj_weight, gain)


def on_device(
    axes,
    layer_argument,
    document_extents,
    distance_bin_lookup,
    tile_location,
    precise_parameter_blocks,
    precise_mean_est,
    precise_variance_est,
    rescaling_coefficients,
    norm_scale_mean_est,
    norm_scale_variance_est,
    distance_bias_table,
    offset_bias_mean_est,
    offset_bias_variance_est,
    sharpness_exponent,
    sharpness_mean_est,
    sharpness_variance_est,
):
    wide, narrow, far, near = axes
    everyone = wide + narrow
    near_axes = near + narrow
    wide_count = lax.axis_size(wide)
    narrow_count = lax.axis_size(narrow)
    far_count = lax.axis_size(far)
    near_count = wide_count // far_count
    wide_index = lax.axis_index(wide)
    narrow_index = lax.axis_index(narrow)
    bits = narrow_bits(narrow_count)
    order = peer_order(narrow_count)
    place_of = jnp.array([order.index(peer) for peer in range(narrow_count)], jnp.int32)
    unit_rows = precise_parameter_blocks.shape[1]
    heads_here = distance_bias_table.shape[1]
    head_size = unit_rows // heads_here
    ffn_units = FF // D
    group = TOK_DEV // narrow_count
    own_slots = wide_index * CAP + jnp.arange(CAP, dtype=jnp.int32)

    every_slot = lax.all_gather(
        precise_parameter_blocks.astype(low_type), wide, axis=0, tiled=True
    )

    def block(u):
        return lax.dynamic_index_in_dim(every_slot, tile_location[u], 0, keepdims=False)

    qkv_weight = jnp.concatenate([block(u) for u in range(3)], axis=0)

    part_rows = D // wide_count

    def unit_order(first_unit):
        rows = jnp.concatenate([block(first_unit + k) for k in range(ffn_units)], axis=0)
        rows = rows.reshape(far_count, near_count, part_rows, D)
        return jnp.swapaxes(rows, 0, 1).reshape(near_count, far_count * part_rows, D)

    crossing = [unit_order(5), block(3), unit_order(5 + ffn_units)]
    for rows in crossing:
        qkv_weight = after(qkv_weight, rows)

    near_index = wide_index % near_count

    def fetch(rows, peer, in_parts):
        if in_parts:
            rows = lax.dynamic_index_in_dim(rows, near_index, 0)
        return swap(rows, narrow, peer)

    evens = bits[1:]
    fetched = [
        [fetch(rows, peer, in_parts) for peer in evens]
        for rows, in_parts in zip(crossing, (True, False, True))
    ]

    def exchanged(pieces):
        return [
            [(near_index, rows)]
            + [(near_index ^ step, swap(rows, near, step)) for step in range(1, near_count)]
            for rows in pieces
        ]

    lengths = document_extents[0]
    seq_ends = jnp.cumsum(lengths)
    positions = jnp.arange(TOK_DEV, dtype=jnp.int32)

    def segments_of(where):
        return jnp.sum((seq_ends[None, :] <= where[:, None]).astype(jnp.int32), axis=1)

    segment_ids = segments_of(positions)
    own_segments = segments_of(narrow_index * group + positions[:group])
    tile_starts = jnp.arange(TOK_DEV // LANE, dtype=jnp.int32) * LANE
    origin = place_of[(tile_starts // group) ^ narrow_index] * group + tile_starts % group

    units = []
    for slot in range(CAP):
        here = tile_location == own_slots[slot]
        unit = jnp.sum(jnp.where(here, jnp.arange(1, here.shape[0] + 1, dtype=jnp.int32), 0)) - 1
        early_unit = jnp.maximum(unit - 5, 0)
        row = jnp.where(unit >= 5, early_unit % ffn_units, jnp.clip(unit, 0, ffn_units - 1))
        column = jnp.where(unit >= 5, 1 - early_unit // ffn_units, 2)
        units += [unit, row, column]
    proj_owner = (tile_location[4] // CAP == wide_index).astype(jnp.float32)
    places = [place_of[g ^ narrow_index] for g in range(narrow_count)]

    beyond = LINES * LANE - LANE - 1 - distance_bin_lookup.shape[0]
    offsets_down = jnp.pad(distance_bin_lookup[::-1], (LANE + 1, beyond), constant_values=-1)
    bucket_onehot = (
        offsets_down[:, None] == jnp.arange(BUCKETS, dtype=jnp.int32)[None, :]
    ).astype(jnp.float32)
    rel_values = jnp.dot(bucket_onehot, distance_bias_table, precision=lax.Precision.HIGHEST).T
    rel_values, origin, proj_owner, *scalars = lax.optimization_barrier(
        (rel_values, origin, proj_owner, *units, *places)
    )
    units, places = scalars[: len(units)], scalars[len(units) :]
    tiles_bias = bias_tiles(rel_values.reshape(heads_here, LINES, LANE))

    all_rows = layer_argument.astype(jnp.float32)
    normed_one = (all_rows * rms_scale(all_rows) * rescaling_coefficients[0]).astype(low_type)
    transposed_rows = times_transposed(qkv_weight, normed_one)
    query_cols = (transposed_rows[:unit_rows] * score_scale).astype(low_type)
    key_cols = transposed_rows[unit_rows : 2 * unit_rows].astype(low_type)
    value_cols = transposed_rows[2 * unit_rows :].astype(low_type)
    spread_weight = jnp.pad(
        qkv_weight[unit_rows:].reshape(2 * heads_here, head_size, D),
        ((0, 0), (0, LANE - head_size), (0, 0)),
    ).reshape(2 * heads_here * LANE, D)
    lane_place = jnp.arange(2 * heads_here * LANE, dtype=jnp.int32) % LANE - head_size
    marks = jnp.logical_or(
        lane_place[None, :] == segment_ids[:, None],
        jnp.logical_and(lane_place >= SEQS_DEV, lane_place < SEQS_DEV + 3)[None, :],
    )
    key_value_rows = (
        times_transposed(normed_one, spread_weight) + marks.astype(jnp.float32)
    ).astype(low_type)
    key_rows = key_value_rows[:, : heads_here * LANE]
    value_rows = key_value_rows[:, heads_here * LANE :]
    row_place = jnp.arange(16, dtype=jnp.int32)[:, None]
    apart = jnp.where(
        jnp.logical_and(row_place < SEQS_DEV, row_place != segment_ids[None, :]), masked_score, 0.0
    ).astype(low_type)
    inner_parts = exchanged(fetched[0])
    query_cols = after(query_cols, fetched[0][0])
    context, context_cols, log_rows = attention_forward(
        0, lengths, origin, query_cols, key_rows, value_cols, apart, tiles_bias
    )

    flat = [rows for pieces in fetched[1:] for rows in pieces]
    inner_flat = [rows for parts in inner_parts for _, rows in parts]
    context, *flat = lax.optimization_barrier((context, *flat, *inner_flat))
    inner_rows = iter(flat[2 * len(evens) :])
    inner_parts = [[(index, next(inner_rows)) for index, _ in parts] for parts in inner_parts]
    outer_parts = exchanged(flat[len(evens) : 2 * len(evens)])

    def in_unit_order(own, parts_of_peers):
        whole = jnp.zeros((near_count, narrow_count, far_count * part_rows, D), low_type)
        pieces = [(0, 0, own), (1, 0, swap(own, narrow, 1))]
        for peer, parts in zip(evens, parts_of_peers):
            for index, rows in parts:
                pieces += [(peer, index, rows), (peer + 1, index, swap(rows, narrow, 1))]
        for peer, index, rows in pieces:
            start = (index, narrow_index ^ peer, 0, 0)
            whole = lax.dynamic_update_slice(whole, rows[:, None], start)
        return whole.reshape(FF, D)

    out_pieces = {0: crossing[1], 1: swap(crossing[1], narrow, 1)}
    for peer, rows in zip(evens, flat[: len(evens)]):
        out_pieces[peer], out_pieces[peer + 1] = rows, swap(rows, narrow, 1)
    out_joined = jnp.concatenate([out_pieces[peer] for peer in order], axis=0)
    inner_joined = in_unit_order(crossing[0], inner_parts)
    outer_joined = in_unit_order(crossing[2], outer_parts)

    def to_peer(values, peer):
        if peer == 0:
            return values
        return swap(values, narrow, peer)

    context_own = jnp.concatenate(
        [
            to_peer(context[s * group : (s + 1) * group], peer)
            for s, peer in enumerate(order)
        ],
        axis=1,
    )
    own_rows = lax.dynamic_slice_in_dim(layer_argument, narrow_index * group, group, 0).astype(
        jnp.float32
    )
    scale_one = rms_scale(own_rows)
    residual_mid = own_rows + plain_product(context_own, out_joined)
    scale_two = rms_scale(residual_mid)
    normed_two = (residual_mid * scale_two * rescaling_coefficients[1]).astype(low_type)

    hidden_low, hidden_slope = gelu_and_slope(times_transposed(normed_two, inner_joined))
    proj_rows = after(block(4), normed_two)
    for bit in reversed(bits):
        came = after(swap(proj_rows, narrow, bit), hidden_low)
        proj_rows = jnp.concatenate([proj_rows, came], axis=0)
    proj_weight = natural_rows(proj_rows, places)
    result_own = residual_mid + plain_product(hidden_low, outer_joined)
    result_low = result_own.astype(low_type)

    scale_three = rms_scale(result_own)
    member = (
        own_segments[None, :] == jnp.arange(SEQS_DEV, dtype=jnp.int32)[:, None]
    ).astype(jnp.float32)
    length_values = lengths.astype(jnp.float32)[:, None]
    unscaled_part = (
        jnp.dot(member, result_own * scale_three, precision=lax.Precision.HIGHEST) / length_values
    )
    total_seqs = wide_count * SEQS_DEV
    own_pooled_grad, loss_low, loss_row, final_gain_grad = contrastive(
        jnp.concatenate([wide_index.reshape(1), lengths]),
        sharpness_exponent,
        spread(unscaled_part, everyone).reshape(total_seqs * narrow_count, D),
        proj_weight,
        rescaling_coefficients[2:3],
        total_seqs,
    )
    loss = loss_row[0, 0]
    sharpness_total = loss_row[0, 1:2]
    proj_grad_own = lax.dynamic_slice_in_dim(
        loss_low[:total_seqs], narrow_index * unit_rows, unit_rows, 1
    )
    proj_weight_grad = outer_product(proj_grad_own, loss_low[total_seqs:])

    weighted = own_pooled_grad[SEQS_DEV - 1]
    for s in range(SEQS_DEV - 2, -1, -1):
        weighted = jnp.where((own_segments == s)[:, None], own_pooled_grad[s], weighted)
    inner_mean = jnp.mean(weighted * result_own, axis=-1, keepdims=True)
    encoded_grad = scale_three * weighted - result_own * (
        scale_three * scale_three * scale_three * inner_mean
    )
    ffn_grad_low = encoded_grad.astype(low_type)
    group_rows = part_rows if part_rows % 16 == 0 else D
    weight_grads, normed_two_grad = feed_forward_backward(
        ffn_grad_low,
        normed_two,
        hidden_low,
        hidden_slope,
        inner_joined,
        outer_joined,
        group_rows,
    )
    near_part = lax.psum_scatter(
        weight_grads.reshape(2 * FF, D), near_axes, scatter_dimension=0, tiled=True
    )
    mid_norm_grad, ffn_gain_grad = norm_backward(
        residual_mid, scale_two, rescaling_coefficients[1], normed_two_grad
    )
    mid_grad = encoded_grad + mid_norm_grad
    attn_grad_low = mid_grad.astype(low_type)

    context_grad_own = times_transposed(attn_grad_low, out_joined).astype(low_type)
    context_grad = [
        to_peer(context_grad_own[:, s * unit_rows : (s + 1) * unit_rows], peer)
        for s, peer in enumerate(order)
    ]
    attn_grad_low = after(attn_grad_low, context_grad_own)
    out_kept = outer_product(context_own, attn_grad_low).astype(low_type)
    for bit in bits:
        half = out_kept.shape[0] // 2
        out_came = swap(out_kept[half:], narrow, bit)
        if bit == bits[-1]:
            break
        out_kept = sum_low(out_kept[:half], out_came)
    context_grad = after(jnp.concatenate(context_grad, axis=0), out_kept)
    qkv_cols, qkv_rows, bias_lines = attention_backward(
        lengths,
        origin,
        query_cols,
        key_rows,
        value_rows,
        key_cols,
        context_grad,
        context_cols,
        log_rows,
        apart,
        tiles_bias,
    )
    qkv_cols, qkv_rows, out_came = lax.optimization_barrier((qkv_cols, qkv_rows, out_came))
    out_grad = sum_low(out_kept[: out_came.shape[0]], out_came)
    offset_bias_slope = lax.dot_general(
        bucket_onehot,
        bias_lines.reshape(heads_here, LINES * LANE),
        (((0,), (1,)), ((), ())),
        precision=lax.Precision.HIGHEST,
    )

    late = jnp.concatenate(
        [plain_product(qkv_cols, normed_one).astype(low_type), out_grad], axis=0
    ).reshape(far_count, near_count, part_rows, D)
    half = qkv_rows.shape[0] // 2
    rows_sent = plain_product(qkv_rows[half:], qkv_weight).astype(low_type)
    rows_kept = plain_product(qkv_rows[:half], after(qkv_weight, rows_sent))
    late_sum = lax.dynamic_index_in_dim(late, near_index, 1, keepdims=False)
    for peer in range(1, near_count):
        sent = lax.dynamic_index_in_dim(late, near_index ^ peer, 1, keepdims=False)
        late_sum = sum_low(late_sum, after(swap(sent, near, peer), rows_kept))
    early = after(near_part, late).reshape(-1, 2, group_rows // part_rows, part_rows, D)
    early = jnp.swapaxes(early, 1, 2).reshape(far_count, 2, part_rows, D)
    terms = jnp.concatenate([early, late_sum[:, None]], axis=1)
    own_part = lax.psum_scatter(
        terms.reshape(far_count * 3 * part_rows, D), far, scatter_dimension=0, tiled=True
    )
    normed_one_grad = rows_kept + swap(rows_sent, narrow, bits[0]).astype(jnp.float32)
    for bit in bits[1:]:
        half = normed_one_grad.shape[0] // 2
        came = swap(normed_one_grad[half:].astype(low_type), narrow, bit)
        normed_one_grad = normed_one_grad[:half] + came.astype(jnp.float32)
    input_norm_grad, attn_gain_grad = norm_backward(
        own_rows, scale_one, rescaling_coefficients[0], normed_one_grad
    )
    input_own = mid_grad + input_norm_grad
    sums = lax.all_gather(after(own_part, input_own), wide, axis=0, tiled=True)
    bias_size = offset_bias_slope.size
    squares = jnp.sum(jnp.square(own_part.astype(jnp.float32))) + proj_owner * jnp.sum(
        jnp.square(proj_weight_grad)
    )
    small = jnp.stack(
        [
            ffn_gain_grad,
            attn_gain_grad,
            jnp.pad(offset_bias_slope.reshape(bias_size), (0, D - bias_size)),
            jnp.broadcast_to(squares, (D,)),
        ]
    )
    small_all = spread(small, everyone).reshape(wide_count, narrow_count, 4, D)
    def gathered(rows, other):
        for bit in reversed(bits):
            came = swap(rows, narrow, bit)
            if bit == bits[-1]:
                came = after(came, other)
            rows = jnp.concatenate([rows, came], axis=0)
        return natural_rows(rows, places).astype(jnp.float32)

    input_grad = gathered(input_own.astype(low_type), small_all)
    layer_result = gathered(after(result_low, input_own), small_all)
    gain_sums = jnp.sum(small_all[:, :, :2], axis=(0, 1))
    gain_total = jnp.stack([gain_sums[1], gain_sums[0], final_gain_grad[0]])
    bias_all = jnp.sum(small_all[:, :, 2], axis=0)
    square_terms = small_all[:, :, 3, 0]
    bias_total = lax.dynamic_index_in_dim(bias_all, narrow_index, 0, keepdims=False)[
        :bias_size
    ].reshape(offset_bias_slope.shape)
    sums, proj_weight_grad, square_terms, *_ = lax.optimization_barrier(
        (sums, proj_weight_grad, square_terms, input_grad, layer_result, gain_total, bias_total)
    )
    sums = sums.reshape(ffn_units, wide_count // ffn_units, 3, part_rows, D)
    slot_grads = []
    for slot in range(CAP):
        unit, row, column = units[3 * slot : 3 * slot + 3]
        low_sum = lax.dynamic_slice(
            sums, (row, 0, column, 0, 0), (1, wide_count // ffn_units, 1, part_rows, D)
        ).reshape(unit_rows, D)
        low_sum = jnp.where(unit == 4, proj_weight_grad, low_sum.astype(jnp.float32))
        slot_grads.append(jnp.where(unit >= 0, low_sum, 0.0))
    slot_grads = jnp.stack(slot_grads)
    grad_norm = jnp.sqrt(
        jnp.sum(square_terms)
        + jnp.sum(gain_total * gain_total)
        + jnp.sum(bias_all * bias_all)
        + jnp.sum(sharpness_total * sharpness_total)
    )
    multiplier = jnp.minimum(1.0, clip_limit / grad_norm)
    slot_first, slot_second, slot_weight = decoupled_decay_step(
        slot_grads,
        precise_mean_est,
        precise_variance_est,
        precise_parameter_blocks,
        multiplier,
        learn_rate,
    )
    gain_first, gain_second, gain_new = decoupled_decay_step(
        gain_total,
        norm_scale_mean_est,
        norm_scale_variance_est,
        rescaling_coefficients,
        multiplier,
        side_rate,
    )
    bias_first, bias_second, bias_new = decoupled_decay_step(
        bias_total,
        offset_bias_mean_est,
        offset_bias_variance_est,
        distance_bias_table,
        multiplier,
        side_rate,
    )
    sharpness_mean_fresh, sharpness_variance_fresh, sharpness_exponent_fresh = decoupled_decay_step(
        sharpness_total,
        sharpness_mean_est,
        sharpness_variance_est,
        sharpness_exponent,
        multiplier,
        learn_rate,
    )
    return (
        loss,
        layer_result,
        input_grad,
        grad_norm,
        slot_first,
        slot_second,
        slot_weight,
        gain_first,
        gain_second,
        gain_new,
        bias_first,
        bias_second,
        bias_new,
        sharpness_mean_fresh,
        sharpness_variance_fresh,
        sharpness_exponent_fresh,
    )


def solution(mesh):
    wide, narrow, far, near = ("wide",), ("narrow",), ("wide",), ()
    if dict(mesh.shape) == {"wide": 8, "narrow": 4}:
        mesh = Mesh(mesh.devices.reshape(4, 2, 2, 2), ("line", "pair", "side", "core"))
        wide, narrow, far, near = ("line", "pair"), ("side", "core"), ("line",), ("pair",)
    whole, rows, blocks, heads = P(), P(wide, None), P(wide, narrow, None), P(None, narrow)
    arguments = (rows, rows, whole, whole, blocks, blocks, blocks, whole, whole, whole)
    arguments += (heads, heads, heads, whole, whole, whole)
    results = (whole, rows, rows, whole, blocks, blocks, blocks, whole, whole, whole)
    results += (heads, heads, heads, whole, whole, whole)

    def body(*arrays):
        return on_device((wide, narrow, far, near), *arrays)

    return jax.shard_map(
        body, mesh=mesh, in_specs=arguments, out_specs=results, check_vma=False
    )
```

profile of v0, /device:TPU:0, one launch (start us, length us, event | category | flops | bytes accessed | tf_op | source)
XLA Modules:
  0.0 484.4 jit_solution(5089269453282245767)
XLA Ops:
  7.3 2.1 convert_element_type.142
  13.4 2.0 fusion.52
  35.7 1.6 convolution_bitcast_fusion
  41.9 5.4 %bias_tiles.1.refs_6_.bias = f32[3,4224,128]{2,1,0:T(8,128)} custom-call(f32[3,18,128]{2,1,0:T(8,128)} %reshape.269.chunks), custom_call_target="tpu_custom_call" | custom-call | tf_op jit(solution)/shard_map/bias_tiles/pallas_call | solution.py:175
  57.1 3.0 fusion
  60.8 32.6 %all-gather.3.cloned.1.call-done = bf16[16,192,768]{2,1,0:T(8,128)(2,1)} async-done(((bf16[2,192,768]{2,1,0:T(8,128)(2,1)}), bf16[16,192,768]{2,1,0:T(8,128)(2,1)}) %all-gather.3.cloned.1.call-update) | async-done | bytes 4718608 | tf_op jit(solution)/shard_map/all_gather | solution.py:567
  93.4 2.3 dynamic-slice_bitcast_fusion.1
  96.1 1.5 collective-permute-start.1
  99.8 2.6 fusion.76
  102.5 4.7 add_convert_fusion.1
  107.2 2.3 fusion.67
  109.6 1.4 fusion.68
  113.3 5.4 %collective-permute-done = bf16[1,384,768]{2,1,0:T(8,128)(2,1)} collective-permute-done((bf16[1,384,768]{2,1,0:T(8,128)(2,1)S(1)}, bf16[1,384,768]{2,1,0:T(8,128)(2,1)}, u32[]{:S(2)}, u32[]{:S(2)}) %collective-permute-start) | collective-permute-done | bytes 589856 | tf_op jit(solution)/shard_map/ppermute | solution.py:82
  119.7 34.3 %attention_forward.1 = (bf16[2560,192]{1,0:T(8,128)(2,1)}, f32[192,2560]{1,0:T(8,128)}, f32[3,2560]{1,0:T(4,128)}) custom-call(s32[4]{0:T(128)} %bitcast.172, s32[20]{0:T(128)} %fusion.50.refs_1_.origin, bf16[192,2560]{1,0:T(8,128)(2,1)} %fusion.12.refs_2_.qT, bf16[2560,384]{1,0:T(8,128)(2,1)} %get-tuple-element.247.refs_3_.kn, ...), custom_call_target="tpu_custom_call" | custom-call | flops 491520 | bytes 491520 | tf_op jit(solution)/shard_map/attention_forward/pallas_call | solution.py:263
  154.1 2.5 bitcast_dynamic-update-slice_fusion
  156.6 1.5 bitcast_dynamic-update-slice_fusion.2
  160.9 1.3 bitcast_dynamic-update-slice_fusion.7
  162.4 6.1 %collective-permute-done.6 = bf16[640,192]{1,0:T(8,128)(2,1)S(1)} collective-permute-done((bf16[640,192]{1,0:T(8,128)(2,1)S(1)}, bf16[640,192]{1,0:T(8,128)(2,1)S(1)}, u32[]{:S(2)}, u32[]{:S(2)}) %collective-permute-start.6) | collective-permute-done | bytes 245792 | tf_op jit(solution)/shard_map/ppermute | solution.py:82
  168.9 6.9 %collective-permute-done.4 = bf16[640,192]{1,0:T(8,128)(2,1)S(1)} collective-permute-done((bf16[640,192]{1,0:T(8,128)(2,1)S(1)}, bf16[640,192]{1,0:T(8,128)(2,1)S(1)}, u32[]{:S(2)}, u32[]{:S(2)}) %collective-permute-start.4) | collective-permute-done | bytes 245792 | tf_op jit(solution)/shard_map/ppermute | solution.py:82
  175.8 2.6 multiply_reduce_fusion.4
  178.8 1.6 collective-permute-start.16
  181.6 8.5 %add_convert_fusion = (bf16[640,3072]{1,0:T(8,128)(2,1)}, bf16[640,3072]{1,0:T(8,128)(2,1)S(1)}) fusion(bf16[640,768]{1,0:T(8,128)(2,1)S(1)} %multiply_convert_fusion.1.rows, bf16[3072,768]{1,0:T(8,128)(2,1)S(1)} %bitcast.150), kind=kOutput, calls=%fused_computation.5 | convolution fusion | flops 3057254400 | bytes 13565952 | tf_op jit(solution)/shard_map/dot_general | solution.py:41
  192.3 3.3 multiply_reduce_fusion.3
  197.9 2.6 all-to-all-start
  203.3 10.4 %all-to-all-done = f32[32,4,768]{2,1,0:T(4,128)S(1)} async-done(((f32[32,4,768]{2,1,0:T(4,128)}), f32[32,4,768]{2,1,0:T(4,128)S(1)}, u32[]{:S(2)}, u32[]{:S(2)}) %all-to-all-start) | async-done | bytes 393248 | tf_op jit(solution)/shard_map/all_to_all | solution.py:136
  214.6 3.9 contrastive.1
  220.1 1.9 fusion.18.grad
  221.9 19.5 %feed_forward_backward.1 = (bf16[32,2,96,768]{3,2,1,0:T(8,128)(2,1)}, f32[640,768]{1,0:T(8,128)}) custom-call(bf16[640,768]{1,0:T(8,128)(2,1)} %fusion.18.grad, bf16[640,768]{1,0:T(8,128)(2,1)} %copy-done.13, bf16[640,3072]{1,0:T(8,128)(2,1)} %copy-done.12, bf16[640,3072]{1,0:T(8,128)(2,1)} %get-tuple-element.223.slope, bf16[3072,768]{1,0:T(8,128)(2,1)} %bitcast.151, ...), custom_call_target="tpu_custom_call" | custom-call | flops 2359296 | bytes 2359296 | tf_op jit(solution)/shard_map/feed_forward_backward/pallas_call | solution.py:434
  241.5 2.8 multiply_reduce_fusion
  244.8 2.7 fusion.66
  247.6 2.1 convolution_convert_fusion.2
  249.7 1.4 convolution_convert_fusion.1
  254.9 6.1 %collective-permute-done.20 = bf16[640,192]{1,0:T(8,128)(2,1)S(1)} collective-permute-done((bf16[640,192]{1,0:T(8,128)(2,1)S(1)}, bf16[640,192]{1,0:T(8,128)(2,1)S(1)}, u32[]{:S(2)}, u32[]{:S(2)}) %collective-permute-start.20) | collective-permute-done | bytes 245792 | tf_op jit(solution)/shard_map/ppermute | solution.py:82
  261.0 9.4 %collective-permute-done.18 = bf16[640,192]{1,0:T(8,128)(2,1)S(1)} collective-permute-done((bf16[640,192]{1,0:T(8,128)(2,1)S(1)}, bf16[640,192]{1,0:T(8,128)(2,1)S(1)}, u32[]{:S(2)}, u32[]{:S(2)}) %collective-permute-start.18) | collective-permute-done | bytes 245792 | tf_op jit(solution)/shard_map/ppermute | solution.py:82
  271.8 48.3 %attention_backward.1 = (bf16[576,2560]{1,0:T(8,128)(2,1)}, bf16[2560,576]{1,0:T(8,128)(2,1)}, f32[3,18,128]{2,1,0:T(8,128)}) custom-call(s32[4]{0:T(128)} %bitcast.174, s32[20]{0:T(128)} %fusion.50.refs_1_.origin, bf16[192,2560]{1,0:T(8,128)(2,1)} %fusion.12.refs_2_.qT, bf16[2560,384]{1,0:T(8,128)(2,1)} %get-tuple-element.247.refs_3_.kn, ...), custom_call_target="tpu_custom_call" | custom-call | flops 491520 | bytes 491520 | tf_op jit(solution)/shard_map/attention_backward/pallas_call | solution.py:384
  320.1 4.6 convolution_convert_fusion
  324.9 2.7 convolution_convert_fusion.3
  327.8 1.7 copy-done.50
  329.5 3.7 fusion.16
  333.1 10.4 %collective-permute-done.26 = bf16[4,96,768]{2,1,0:T(8,128)(2,1)S(1)} collective-permute-done((bf16[4,96,768]{2,1,0:T(8,128)(2,1)S(1)}, bf16[4,96,768]{2,1,0:T(8,128)(2,1)S(1)}, u32[]{:S(2)}, u32[]{:S(2)}) %collective-permute-start.26) | collective-permute-done | bytes 589856 | tf_op jit(solution)/shard_map/ppermute | solution.py:82
  343.7 2.6 pad_maximum_fusion.3
  346.4 3.3 convert_add_fusion
  349.8 1.9 copy-done
  352.2 1.5 fusion.3
  354.9 20.1 %collective-permute-done.24 = bf16[640,768]{1,0:T(8,128)(2,1)S(1)} collective-permute-done((bf16[640,768]{1,0:T(8,128)(2,1)S(1)}, bf16[640,768]{1,0:T(8,128)(2,1)S(1)}, u32[]{:S(2)}, u32[]{:S(2)}) %collective-permute-start.24) | collective-permute-done | bytes 983072 | tf_op jit(solution)/shard_map/ppermute | solution.py:82
  375.0 2.7 fusion.11
  377.7 2.6 fusion.8
  381.3 1.8 multiply_reduce_fusion.6
  383.8 1.9 fusion.26
  385.8 1.5 collective-permute-start.25
  387.3 1.8 multiply_reduce_fusion.5
  391.4 3.6 all-to-all-start.1
  395.0 1.8 collective-permute-start.28
  396.8 17.1 %collective-permute-done.25 = bf16[640,768]{1,0:T(8,128)(2,1)S(1)} collective-permute-done((bf16[640,768]{1,0:T(8,128)(2,1)S(1)}, bf16[640,768]{1,0:T(8,128)(2,1)S(1)}, u32[]{:S(2)}, u32[]{:S(2)}) %collective-permute-start.25) | collective-permute-done | bytes 983072 | tf_op jit(solution)/shard_map/ppermute | solution.py:82
  414.0 2.9 all-to-all-done.1
  416.9 1.4 pad_maximum_fusion.1
  418.3 16.2 %collective-permute-done.28 = bf16[640,768]{1,0:T(8,128)(2,1)} collective-permute-done((bf16[640,768]{1,0:T(8,128)(2,1)S(1)}, bf16[640,768]{1,0:T(8,128)(2,1)}, u32[]{:S(2)}, u32[]{:S(2)}) %collective-permute-start.28) | collective-permute-done | bytes 983072 | tf_op jit(solution)/shard_map/ppermute | solution.py:82
  434.6 2.7 pad_maximum_fusion.2
  449.6 2.9 constant_dynamic-update-slice_fusion.3
  452.6 2.3 constant_dynamic-slice_fusion.10
  454.9 2.0 pad_maximum_fusion
  457.2 3.5 maximum_convert_fusion
  460.7 3.5 maximum_convert_fusion.1
  470.4 2.5 multiply_subtract_fusion.1
  (279 shorter events, 47.6 us)
Async XLA Ops:
  7.2 27.3 %copy-start.41 = (s32[4]{0:T(128)S(1)}, s32[4]{0:T(128)}, u32[]{:S(2)}) copy-start(s32[4]{0:T(128)} %constant.255.clone) | copy-start | bytes 52
  7.2 27.0 %copy-start.42 = (s32[2047]{0:T(1024)S(1)}, s32[2047]{0:T(1024)}, u32[]{:S(2)}) copy-start(s32[2047]{0:T(1024)} %param.19) | copy-start | bytes 24568
  7.2 28.5 %copy-start.45 = (f32[32,3]{0,1:T(4,128)S(1)}, f32[32,3]{0,1:T(4,128)}, u32[]{:S(2)}) copy-start(f32[32,3]{0,1:T(4,128)} %param.27) | copy-start | bytes 1156
  7.2 33.9 %copy-start.43 = (s32[1,4]{1,0:T(1,128)S(1)}, s32[1,4]{1,0:T(1,128)}, u32[]{:S(2)}) copy-start(s32[1,4]{1,0:T(1,128)} %param.18) | copy-start | bytes 52
  7.2 86.2 %all-gather.3.cloned.1.call-start = ((), (), s32[]{:S(2)}) async-start(), calls=%async_computation.4 | async-start | bytes 5308416 | tf_op jit(solution)/shard_map/all_gather | solution.py:567
  34.4 13.0 %copy-start.36 = (s32[2304]{0:T(1024)}, s32[2304]{0:T(1024)S(1)}, u32[]{:S(2)}) copy-start(s32[2304]{0:T(1024)S(1)} %pad.12) | copy-start | bytes 27652
  41.9 14.6 %copy-start.25 = (f32[3,768]{1,0:T(4,128)S(1)}, f32[3,768]{1,0:T(4,128)}, u32[]{:S(2)}) copy-start(f32[3,768]{1,0:T(4,128)} %param.24) | copy-start | bytes 27652
  57.1 45.4 %copy-start.27 = (f32[768]{0:T(1024)}, f32[768]{0:T(1024)S(1)}, u32[]{:S(2)}) copy-start(f32[768]{0:T(1024)S(1)} %get-tuple-element.209) | copy-start | bytes 9220
  60.1 42.4 %copy-start.34 = (f32[2560]{0:T(1024)}, f32[2560]{0:T(1024)S(1)}, u32[]{:S(2)}) copy-start(f32[2560]{0:T(1024)S(1)} %add_rsqrt_fusion) | copy-start | bytes 30724
  95.7 80.1 %copy-start.21 = (bf16[192,768]{1,0:T(8,128)(2,1)}, bf16[192,768]{1,0:T(8,128)(2,1)S(1)}, u32[]{:S(2)}) copy-start(bf16[192,768]{1,0:T(8,128)(2,1)S(1)} %get-tuple-element.230) | copy-start | bytes 884740
  95.9 60.7 %collective-permute-start.9 = (bf16[2,384,768]{2,1,0:T(8,128)(2,1)S(1)}, bf16[2,384,768]{2,1,0:T(8,128)(2,1)}, u32[]{:S(2)}, u32[]{:S(2)}) collective-permute-start(bf16[2,384,768]{2,1,0:T(8,128)(2,1)S(1)} %bitcast.155), channel_id=1, source_target_pairs={{0,1},{1,0},{2,3},{3,2},{4,5},{5,4},{6,7},{7,6},{8,9},{9,8},{10,11... | collective-permute-start | bytes 3538952 | tf_op jit(solution)/shard_map/ppermute | solution.py:82
  96.1 62.0 %collective-permute-start.1 = (bf16[192,768]{1,0:T(8,128)(2,1)S(1)}, bf16[192,768]{1,0:T(8,128)(2,1)}, u32[]{:S(2)}, u32[]{:S(2)}) collective-permute-start(bf16[192,768]{1,0:T(8,128)(2,1)S(1)} %get-tuple-element.230), channel_id=1, source_target_pairs={{0,2},{1,3},{2,0},{3,1},{4,6},{5,7},{6,4},{7,5},{8,10},{9,11},{10,... | collective-permute-start | bytes 884744 | tf_op jit(solution)/shard_map/ppermute | solution.py:82
  97.8 56.2 %collective-permute-start.12 = (bf16[2,384,768]{2,1,0:T(8,128)(2,1)S(1)}, bf16[2,384,768]{2,1,0:T(8,128)(2,1)}, u32[]{:S(2)}, u32[]{:S(2)}) collective-permute-start(bf16[2,384,768]{2,1,0:T(8,128)(2,1)S(1)} %bitcast.158), channel_id=1, source_target_pairs={{0,1},{1,0},{2,3},{3,2},{4,5},{5,4},{6,7},{7,6},{8,9},{9,8},{10,11... | collective-permute-start | bytes 3538952 | tf_op jit(solution)/shard_map/ppermute | solution.py:82
  98.1 20.6 %collective-permute-start = (bf16[1,384,768]{2,1,0:T(8,128)(2,1)S(1)}, bf16[1,384,768]{2,1,0:T(8,128)(2,1)}, u32[]{:S(2)}, u32[]{:S(2)}) collective-permute-start(bf16[1,384,768]{2,1,0:T(8,128)(2,1)S(1)} %constant_dynamic-slice_fusion.16), channel_id=1, source_target_pairs={{0,2},{1,3},{2,0},{3,1},{4,6},{5,7},{6,4},{7,5},{8,10},{9,11},{10,... | collective-permute-start | bytes 1769480 | tf_op jit(solution)/shard_map/ppermute | solution.py:82
  111.0 47.1 %collective-permute-start.2 = (bf16[1,384,768]{2,1,0:T(8,128)(2,1)S(1)}, bf16[1,384,768]{2,1,0:T(8,128)(2,1)}, u32[]{:S(2)}, u32[]{:S(2)}) collective-permute-start(bf16[1,384,768]{2,1,0:T(8,128)(2,1)S(1)} %constant_dynamic-slice_fusion.15), channel_id=1, source_target_pairs={{0,2},{1,3},{2,0},{3,1},{4,6},{5,7},{6,4},{7,5},{8,10},{9,11},{10,... | collective-permute-start | bytes 1769480 | tf_op jit(solution)/shard_map/ppermute | solution.py:82
  112.1 7.5 %copy-start.3 = (bf16[2,4,384,768]{3,2,1,0:T(8,128)(2,1)}, bf16[2,4,384,768]{3,2,1,0:T(8,128)(2,1)S(1)}, u32[]{:S(2)}) copy-start(bf16[2,4,384,768]{3,2,1,0:T(8,128)(2,1)S(1)} %bitcast_dynamic-update-slice_fusion.1) | copy-start | bytes 14155780
  118.7 39.4 %collective-permute-start.3 = (bf16[1,384,768]{2,1,0:T(8,128)(2,1)}, bf16[1,384,768]{2,1,0:T(8,128)(2,1)}, u32[]{:S(2)}, u32[]{:S(2)}) collective-permute-start(bf16[1,384,768]{2,1,0:T(8,128)(2,1)} %collective-permute-done), channel_id=1, source_target_pairs={{0,4},{4,0},{1,5},{5,1},{2,6},{6,2},{3,7},{7,3},{8,12},{12,8},{9,1... | collective-permute-start | bytes 1769480 | tf_op jit(solution)/shard_map/ppermute | solution.py:82
  154.0 8.2 %collective-permute-start.7 = (bf16[192,768]{1,0:T(8,128)(2,1)S(1)}, bf16[192,768]{1,0:T(8,128)(2,1)S(1)}, u32[]{:S(2)}, u32[]{:S(2)}) collective-permute-start(bf16[192,768]{1,0:T(8,128)(2,1)S(1)} %get-tuple-element.230), channel_id=1, source_target_pairs={{0,1},{1,0},{2,3},{3,2},{4,5},{5,4},{6,7},{7,6},{8,9},{9,8},{10,11... | collective-permute-start | bytes 884744 | tf_op jit(solution)/shard_map/ppermute | solution.py:82
  158.1 17.7 %collective-permute-start.8 = (bf16[192,768]{1,0:T(8,128)(2,1)}, bf16[192,768]{1,0:T(8,128)(2,1)S(1)}, u32[]{:S(2)}, u32[]{:S(2)}) collective-permute-start(bf16[192,768]{1,0:T(8,128)(2,1)} %collective-permute-done.1), channel_id=1, source_target_pairs={{0,1},{1,0},{2,3},{3,2},{4,5},{5,4},{6,7},{7,6},{8,9},{9,8},{10,11... | collective-permute-start | bytes 884744 | tf_op jit(solution)/shard_map/ppermute | solution.py:82
  158.7 19.8 %copy-start.19 = (bf16[640,192]{1,0:T(8,128)(2,1)}, bf16[640,192]{1,0:T(8,128)(2,1)S(1)}, u32[]{:S(2)}) copy-start(bf16[640,192]{1,0:T(8,128)(2,1)S(1)} %get-tuple-element.253) | copy-start | bytes 737284
  158.7 9.8 %collective-permute-start.6 = (bf16[640,192]{1,0:T(8,128)(2,1)S(1)}, bf16[640,192]{1,0:T(8,128)(2,1)S(1)}, u32[]{:S(2)}, u32[]{:S(2)}) collective-permute-start(bf16[640,192]{1,0:T(8,128)(2,1)S(1)} %get-tuple-element.254), channel_id=1, source_target_pairs={{0,3},{1,2},{2,1},{3,0},{4,7},{5,6},{6,5},{7,4},{8,11},{9,10},{10,... | collective-permute-start | bytes 737288 | tf_op jit(solution)/shard_map/ppermute | solution.py:82
  160.0 8.9 %collective-permute-start.5 = (bf16[640,192]{1,0:T(8,128)(2,1)S(1)}, bf16[640,192]{1,0:T(8,128)(2,1)S(1)}, u32[]{:S(2)}, u32[]{:S(2)}) collective-permute-start(bf16[640,192]{1,0:T(8,128)(2,1)S(1)} %get-tuple-element.255), channel_id=1, source_target_pairs={{0,1},{1,0},{2,3},{3,2},{4,5},{5,4},{6,7},{7,6},{8,9},{9,8},{10,11... | collective-permute-start | bytes 737288 | tf_op jit(solution)/shard_map/ppermute | solution.py:82
  160.4 15.4 %collective-permute-start.4 = (bf16[640,192]{1,0:T(8,128)(2,1)S(1)}, bf16[640,192]{1,0:T(8,128)(2,1)S(1)}, u32[]{:S(2)}, u32[]{:S(2)}) collective-permute-start(bf16[640,192]{1,0:T(8,128)(2,1)S(1)} %get-tuple-element.256), channel_id=1, source_target_pairs={{0,2},{1,3},{2,0},{3,1},{4,6},{5,7},{6,4},{7,5},{8,10},{9,11},{10,... | collective-permute-start | bytes 737288 | tf_op jit(solution)/shard_map/ppermute | solution.py:82
  162.3 16.2 %copy-start.58 = (bf16[192,768]{1,0:T(8,128)(2,1)}, bf16[192,768]{1,0:T(8,128)(2,1)S(1)}, u32[]{:S(2)}) copy-start(bf16[192,768]{1,0:T(8,128)(2,1)S(1)} %collective-permute-done.7) | copy-start | bytes 884740
  162.3 18.1 %collective-permute-start.10 = (bf16[1,384,768]{2,1,0:T(8,128)(2,1)}, bf16[1,384,768]{2,1,0:T(8,128)(2,1)S(1)}, u32[]{:S(2)}, u32[]{:S(2)}) collective-permute-start(bf16[1,384,768]{2,1,0:T(8,128)(2,1)} %collective-permute-done), channel_id=1, source_target_pairs={{0,1},{1,0},{2,3},{3,2},{4,5},{5,4},{6,7},{7,6},{8,9},{9,8},{10,11... | collective-permute-start | bytes 1769480 | tf_op jit(solution)/shard_map/ppermute | solution.py:82
  168.5 10.0 %copy-start.52 = (bf16[640,192]{1,0:T(8,128)(2,1)}, bf16[640,192]{1,0:T(8,128)(2,1)S(1)}, u32[]{:S(2)}) copy-start(bf16[640,192]{1,0:T(8,128)(2,1)S(1)} %collective-permute-done.6) | copy-start | bytes 737284
  168.5 23.4 %collective-permute-start.13 = (bf16[1,384,768]{2,1,0:T(8,128)(2,1)}, bf16[1,384,768]{2,1,0:T(8,128)(2,1)S(1)}, u32[]{:S(2)}, u32[]{:S(2)}) collective-permute-start(bf16[1,384,768]{2,1,0:T(8,128)(2,1)} %collective-permute-done.2), channel_id=1, source_target_pairs={{0,1},{1,0},{2,3},{3,2},{4,5},{5,4},{6,7},{7,6},{8,9},{9,8},{10,11... | collective-permute-start | bytes 1769480 | tf_op jit(solution)/shard_map/ppermute | solution.py:82
  168.9 9.6 %copy-start.54 = (bf16[640,192]{1,0:T(8,128)(2,1)}, bf16[640,192]{1,0:T(8,128)(2,1)S(1)}, u32[]{:S(2)}) copy-start(bf16[640,192]{1,0:T(8,128)(2,1)S(1)} %collective-permute-done.5) | copy-start | bytes 737284
  168.9 21.2 %collective-permute-start.14 = (bf16[1,384,768]{2,1,0:T(8,128)(2,1)}, bf16[1,384,768]{2,1,0:T(8,128)(2,1)S(1)}, u32[]{:S(2)}, u32[]{:S(2)}) collective-permute-start(bf16[1,384,768]{2,1,0:T(8,128)(2,1)} %collective-permute-done.2), channel_id=1, source_target_pairs={{0,4},{4,0},{1,5},{5,1},{2,6},{6,2},{3,7},{7,3},{8,12},{12,8},{9,1... | collective-permute-start | bytes 1769480 | tf_op jit(solution)/shard_map/ppermute | solution.py:82
  175.8 5.7 %collective-permute-start.11 = (bf16[1,384,768]{2,1,0:T(8,128)(2,1)}, bf16[1,384,768]{2,1,0:T(8,128)(2,1)S(1)}, u32[]{:S(2)}, u32[]{:S(2)}) collective-permute-start(bf16[1,384,768]{2,1,0:T(8,128)(2,1)} %collective-permute-done.3), channel_id=1, source_target_pairs={{0,1},{1,0},{2,3},{3,2},{4,5},{5,4},{6,7},{7,6},{8,9},{9,8},{10,11... | collective-permute-start | bytes 1769480 | tf_op jit(solution)/shard_map/ppermute | solution.py:82
  178.5 13.7 %copy-start.6 = (f32[640,768]{1,0:T(8,128)}, f32[640,768]{1,0:T(8,128)S(1)}, u32[]{:S(2)}) copy-start(f32[640,768]{1,0:T(8,128)S(1)} %get-tuple-element.297) | copy-start | bytes 5898244
  178.8 11.3 %copy-start.13 = (bf16[640,768]{1,0:T(8,128)(2,1)}, bf16[640,768]{1,0:T(8,128)(2,1)S(1)}, u32[]{:S(2)}) copy-start(bf16[640,768]{1,0:T(8,128)(2,1)S(1)} %multiply_convert_fusion.1.rows) | copy-start | bytes 2949124
  178.8 11.3 %collective-permute-start.16 = (bf16[192,768]{1,0:T(8,128)(2,1)S(1)}, bf16[192,768]{1,0:T(8,128)(2,1)S(1)}, u32[]{:S(2)}, u32[]{:S(2)}) collective-permute-start(bf16[192,768]{1,0:T(8,128)(2,1)S(1)} %get-tuple-element.80), channel_id=1, source_target_pairs={{0,2},{1,3},{2,0},{3,1},{4,6},{5,7},{6,4},{7,5},{8,10},{9,11},{10,... | collective-permute-start | bytes 884744 | tf_op jit(solution)/shard_map/ppermute | solution.py:82
  181.6 8.5 %copy-start.2 = (bf16[2,4,384,768]{3,2,1,0:T(8,128)(2,1)}, bf16[2,4,384,768]{3,2,1,0:T(8,128)(2,1)S(1)}, u32[]{:S(2)}) copy-start(bf16[2,4,384,768]{3,2,1,0:T(8,128)(2,1)S(1)} %bitcast_dynamic-update-slice_fusion.8) | copy-start | bytes 14155780
  190.1 2.1 collective-permute-start.15
  191.3 10.7 %collective-permute-start.17 = (bf16[384,768]{1,0:T(8,128)(2,1)}, bf16[384,768]{1,0:T(8,128)(2,1)S(1)}, u32[]{:S(2)}, u32[]{:S(2)}) collective-permute-start(bf16[384,768]{1,0:T(8,128)(2,1)} %pad_maximum_fusion.12), channel_id=1, source_target_pairs={{0,1},{1,0},{2,3},{3,2},{4,5},{5,4},{6,7},{7,6},{8,9},{9,8},{10,11... | collective-permute-start | bytes 1769480 | tf_op jit(solution)/shard_map/ppermute | solution.py:82
  197.9 15.8 %all-to-all-start = ((f32[32,4,768]{2,1,0:T(4,128)}), f32[32,4,768]{2,1,0:T(4,128)S(1)}, u32[]{:S(2)}, u32[]{:S(2)}) async-start(f32[32,4,768]{2,1,0:T(4,128)} %broadcast_in_dim.137), calls=%async_computation | async-start | bytes 786432 | tf_op jit(solution)/shard_map/all_to_all | solution.py:136
  200.5 143.2 %reduce-scatter.3.cloned.1.call-start = ((), (), s32[]{:S(2)}) async-start(), calls=%async_computation.5 | async-start | bytes 10616832 | tf_op jit(solution)/shard_map/reduce_scatter | solution.py:768
  202.2 17.2 %copy-start.31 = (pred[640]{0:T(1024)(128)(4,1)S(1)}, pred[640]{0:T(1024)(128)(4,1)}, u32[]{:S(2)}) copy-start(pred[640]{0:T(1024)(128)(4,1)} %get-tuple-element.270) | copy-start | bytes 1924
  202.2 17.2 %copy-start.32 = (pred[640]{0:T(1024)(128)(4,1)S(1)}, pred[640]{0:T(1024)(128)(4,1)}, u32[]{:S(2)}) copy-start(pred[640]{0:T(1024)(128)(4,1)} %get-tuple-element.271) | copy-start | bytes 1924
  202.2 17.2 %copy-start.33 = (pred[640]{0:T(1024)(128)(4,1)S(1)}, pred[640]{0:T(1024)(128)(4,1)}, u32[]{:S(2)}) copy-start(pred[640]{0:T(1024)(128)(4,1)} %get-tuple-element.272) | copy-start | bytes 1924
  241.4 139.8 %reduce-scatter.5.cloned.1.call-start = ((), (), s32[]{:S(2)}) async-start(), calls=%async_computation.6 | async-start | bytes 2211840 | tf_op jit(solution)/shard_map/reduce_scatter | solution.py:826
  251.2 2.6 collective-permute-start.21
  251.6 9.5 %collective-permute-start.20 = (bf16[640,192]{1,0:T(8,128)(2,1)S(1)}, bf16[640,192]{1,0:T(8,128)(2,1)S(1)}, u32[]{:S(2)}, u32[]{:S(2)}) collective-permute-start(bf16[640,192]{1,0:T(8,128)(2,1)S(1)} %get-tuple-element.262), channel_id=1, source_target_pairs={{0,3},{1,2},{2,1},{3,0},{4,7},{5,6},{6,5},{7,4},{8,11},{9,10},{10,... | collective-permute-start | bytes 737288 | tf_op jit(solution)/shard_map/ppermute | solution.py:82
  252.1 8.9 %collective-permute-start.19 = (bf16[640,192]{1,0:T(8,128)(2,1)S(1)}, bf16[640,192]{1,0:T(8,128)(2,1)S(1)}, u32[]{:S(2)}, u32[]{:S(2)}) collective-permute-start(bf16[640,192]{1,0:T(8,128)(2,1)S(1)} %get-tuple-element.263), channel_id=1, source_target_pairs={{0,1},{1,0},{2,3},{3,2},{4,5},{5,4},{6,7},{7,6},{8,9},{9,8},{10,11... | collective-permute-start | bytes 737288 | tf_op jit(solution)/shard_map/ppermute | solution.py:82
  252.6 17.8 %collective-permute-start.18 = (bf16[640,192]{1,0:T(8,128)(2,1)S(1)}, bf16[640,192]{1,0:T(8,128)(2,1)S(1)}, u32[]{:S(2)}, u32[]{:S(2)}) collective-permute-start(bf16[640,192]{1,0:T(8,128)(2,1)S(1)} %get-tuple-element.264), channel_id=1, source_target_pairs={{0,2},{1,3},{2,0},{3,1},{4,6},{5,7},{6,4},{7,5},{8,10},{9,11},{10,... | collective-permute-start | bytes 737288 | tf_op jit(solution)/shard_map/ppermute | solution.py:82
  253.9 66.1 %collective-permute-start.22 = (bf16[192,768]{1,0:T(8,128)(2,1)S(1)}, bf16[192,768]{1,0:T(8,128)(2,1)S(1)}, u32[]{:S(2)}, u32[]{:S(2)}) collective-permute-start(bf16[192,768]{1,0:T(8,128)(2,1)S(1)} %slice.243), channel_id=1, source_target_pairs={{0,2},{1,3},{2,0},{3,1},{4,6},{5,7},{6,4},{7,5},{8,10},{9,11},{10,... | collective-permute-start | bytes 884744 | tf_op jit(solution)/shard_map/ppermute | solution.py:82
  271.8 48.3 %copy-start.15 = (bf16[576,768]{1,0:T(8,128)(2,1)S(1)}, bf16[576,768]{1,0:T(8,128)(2,1)}, u32[]{:S(2)}) copy-start(bf16[576,768]{1,0:T(8,128)(2,1)} %copy-done.14) | copy-start | bytes 2654212
  324.8 21.6 %collective-permute-start.23 = (bf16[1280,768]{1,0:T(8,128)(2,1)}, bf16[1280,768]{1,0:T(8,128)(2,1)}, u32[]{:S(2)}, u32[]{:S(2)}) collective-permute-start(bf16[1280,768]{1,0:T(8,128)(2,1)} %convolution_convert_fusion), channel_id=1, source_target_pairs={{0,1},{1,0},{2,3},{3,2},{4,5},{5,4},{6,7},{7,6},{8,9},{9,8},{10,11... | collective-permute-start | bytes 5898248 | tf_op jit(solution)/shard_map/ppermute | solution.py:82
  327.7 15.8 %collective-permute-start.26 = (bf16[4,96,768]{2,1,0:T(8,128)(2,1)S(1)}, bf16[4,96,768]{2,1,0:T(8,128)(2,1)S(1)}, u32[]{:S(2)}, u32[]{:S(2)}) collective-permute-start(bf16[4,96,768]{2,1,0:T(8,128)(2,1)S(1)} %dynamic-slice_bitcast_fusion), channel_id=1, source_target_pairs={{0,4},{4,0},{1,5},{5,1},{2,6},{6,2},{3,7},{7,3},{8,12},{12,8},{9,1... | collective-permute-start | bytes 1769480 | tf_op jit(solution)/shard_map/ppermute | solution.py:82
  346.4 117.9 %all-gather.5.cloned.1.call-start = ((), (), s32[]{:S(2)}) async-start(), calls=%async_computation.7 | async-start | bytes 3981312 | tf_op jit(solution)/shard_map/all_gather | solution.py:838
  351.8 23.2 %collective-permute-start.24 = (bf16[640,768]{1,0:T(8,128)(2,1)S(1)}, bf16[640,768]{1,0:T(8,128)(2,1)S(1)}, u32[]{:S(2)}, u32[]{:S(2)}) collective-permute-start(bf16[640,768]{1,0:T(8,128)(2,1)S(1)} %slice.280), channel_id=1, source_target_pairs={{0,2},{1,3},{2,0},{3,1},{4,6},{5,7},{6,4},{7,5},{8,10},{9,11},{10,... | collective-permute-start | bytes 2949128 | tf_op jit(solution)/shard_map/ppermute | solution.py:82
  354.9 22.8 %copy-start.1 = (f32[1280,768]{1,0:T(8,128)S(1)}, f32[1280,768]{1,0:T(8,128)}, u32[]{:S(2)}) copy-start(f32[1280,768]{1,0:T(8,128)} %copy-done) | copy-start | bytes 11796484
  385.8 28.2 %collective-permute-start.25 = (bf16[640,768]{1,0:T(8,128)(2,1)S(1)}, bf16[640,768]{1,0:T(8,128)(2,1)S(1)}, u32[]{:S(2)}, u32[]{:S(2)}) collective-permute-start(bf16[640,768]{1,0:T(8,128)(2,1)S(1)} %get-tuple-element.98), channel_id=1, source_target_pairs={{0,2},{1,3},{2,0},{3,1},{4,6},{5,7},{6,4},{7,5},{8,10},{9,11},{10,... | collective-permute-start | bytes 2949128 | tf_op jit(solution)/shard_map/ppermute | solution.py:82
  391.4 25.5 %all-to-all-start.1 = ((f32[32,4,768]{2,1,0:T(4,128)}), f32[32,4,768]{2,1,0:T(4,128)}, u32[]{:S(2)}, u32[]{:S(2)}) async-start(f32[32,4,768]{2,1,0:T(4,128)} %broadcast_in_dim.146), calls=%async_computation.3 | async-start | bytes 786432 | tf_op jit(solution)/shard_map/all_to_all | solution.py:136
  395.0 39.5 %collective-permute-start.28 = (bf16[640,768]{1,0:T(8,128)(2,1)S(1)}, bf16[640,768]{1,0:T(8,128)(2,1)}, u32[]{:S(2)}, u32[]{:S(2)}) collective-permute-start(bf16[640,768]{1,0:T(8,128)(2,1)S(1)} %fusion.8), channel_id=1, source_target_pairs={{0,2},{1,3},{2,0},{3,1},{4,6},{5,7},{6,4},{7,5},{8,10},{9,11},{10,... | collective-permute-start | bytes 2949128 | tf_op jit(solution)/shard_map/ppermute | solution.py:82
  418.3 22.8 %copy-start.44 = (f32[1,128]{1,0:T(1,128)S(1)}, f32[1,128]{1,0:T(1,128)}, u32[]{:S(2)}) copy-start(f32[1,128]{1,0:T(1,128)} %get-tuple-element.87) | copy-start | bytes 1540
  418.3 31.3 %collective-permute-start.27 = (bf16[1280,768]{1,0:T(8,128)(2,1)}, bf16[1280,768]{1,0:T(8,128)(2,1)}, u32[]{:S(2)}, u32[]{:S(2)}) collective-permute-start(bf16[1280,768]{1,0:T(8,128)(2,1)} %pad_maximum_fusion.1), channel_id=1, source_target_pairs={{0,1},{1,0},{2,3},{3,2},{4,5},{5,4},{6,7},{7,6},{8,9},{9,8},{10,11... | collective-permute-start | bytes 5898248 | tf_op jit(solution)/shard_map/ppermute | solution.py:82
  437.3 10.1 %copy-start.40 = (f32[1,768]{1,0:T(1,128)S(1)}, f32[1,768]{1,0:T(1,128)}, u32[]{:S(2)}) copy-start(f32[1,768]{1,0:T(1,128)} %get-tuple-element.110) | copy-start | bytes 9220
  437.3 17.7 %collective-permute-start.29 = (bf16[1280,768]{1,0:T(8,128)(2,1)}, bf16[1280,768]{1,0:T(8,128)(2,1)}, u32[]{:S(2)}, u32[]{:S(2)}) collective-permute-start(bf16[1280,768]{1,0:T(8,128)(2,1)} %pad_maximum_fusion.2), channel_id=1, source_target_pairs={{0,1},{1,0},{2,3},{3,2},{4,5},{5,4},{6,7},{7,6},{8,9},{9,8},{10,11... | collective-permute-start | bytes 5898248 | tf_op jit(solution)/shard_map/ppermute | solution.py:82
  460.7 7.2 %copy-start.39 = (f32[3,768]{1,0:T(4,128)S(1)}, f32[3,768]{1,0:T(4,128)}, u32[]{:S(2)}) copy-start(f32[3,768]{1,0:T(4,128)} %param.25) | copy-start | bytes 27652
  460.7 7.8 %copy-start.46 = (f32[32,3]{0,1:T(4,128)S(1)}, f32[32,3]{0,1:T(4,128)}, u32[]{:S(2)}) copy-start(f32[32,3]{0,1:T(4,128)} %param.27) | copy-start | bytes 1156
  460.7 7.8 %copy-start.47 = (f32[32,3]{0,1:T(4,128)S(1)}, f32[32,3]{0,1:T(4,128)}, u32[]{:S(2)}) copy-start(f32[32,3]{0,1:T(4,128)} %param.29) | copy-start | bytes 1156
  460.7 7.8 %copy-start.48 = (f32[32,3]{0,1:T(4,128)S(1)}, f32[32,3]{0,1:T(4,128)}, u32[]{:S(2)}) copy-start(f32[32,3]{0,1:T(4,128)} %param.28) | copy-start | bytes 1156
  (34 other events, 121.4 us)
Sparse Core Ops, SparseCore 0:
  10.8 82.5 all-gather.2
  241.6 79.7 reduce-scatter.2
  346.5 34.7 reduce-scatter.4
  383.5 72.6 all-gather.4
where the time goes:
time: 491 us; the launch traced here: 484 us
  waiting for transfers between devices  145 us (30%)
  Pallas kernels  111 us (23%)
  between operations  62.5 us (13%)
  other arithmetic  60.9 us (12%)
  matrix products  42.4 us (9%)
  local copies, waits for them, and re-layouts  39.3 us (8%)
  starting transfers between devices  22.8 us (5%)
    ppermute x30, waiting for transfers between devices, swap(): return lax.ppermute(values, axes, [(i, i ^ bit) for i in range(count)])  98.1 us
    pallas_call x1, Pallas kernels, attention_backward(): pl.pallas_call(backward_kernel, out_shape=(jax.ShapeDtypeStruct((3 * widt...  48.3 us
    pallas_call x1, Pallas kernels, attention_forward(): pl.pallas_call(body, out_shape=(jax.ShapeDtypeStruct((rows_here, width),...  34.3 us
    all_gather x1, waiting for transfers between devices, on_device(): lax.all_gather(precise_parameter_blocks.astype(low_type), wide, axis=0, t...  32.6 us
    pallas_call x1, Pallas kernels, feed_forward_backward(): pl.pallas_call(feed_forward_backward_kernel, grid=(FF // UNIT_BLOCK,), ou...  19.5 us
    dot_general x4, matrix products, times_transposed(): lax.dot_general(left_side, right_side, (((1,), (1,)), ((), ())), preferre...  17.9 us
    dot_general x5, matrix products, plain_product(): return jnp.dot(left_side, right_side, preferred_element_type=jnp.float32)  16.9 us
    ppermute x30, starting transfers between devices, swap(): return lax.ppermute(values, axes, [(i, i ^ bit) for i in range(count)])  16.3 us
  transfers between devices with their start and end apart: 36, of which 14 were waited for; matrix products, arithmetic and copies ran while one was open for 25% of the time, Pallas kernels for 18%

commit v1 on v0

--- a/solution.py
+++ b/solution.py
@@ -202,10 +202,13 @@
     )
 
 
-def forward_kernel(first_row, lengths, origin, qT, kn, vT, apart, bias, ctx_o, ctxT_o, lse_o, qa, acc):
-    width, rows_here = qT.shape
+def forward_kernel(
+    lengths, origin, cols, rows_in, apart, bias, ctx_o, ctxT_o, lse_o, qa, acc
+):
+    width, rows_here = cols.shape[0] // 3, cols.shape[1]
     heads = bias.shape[0]
     size = width // heads
+    first_row = 0
     qa[...] = jnp.zeros_like(qa)
 
     @pl.loop(0, rows_here // BQ)
@@ -213,7 +216,8 @@
         q0 = pl.multiple_of(i * BQ, BQ)
         here = pl.ds(q0, BQ)
         for h in range(heads):
-            qa[h * LANE : h * LANE + size, :] = qT[h * size : (h + 1) * size, here]
+            scaled = cols[h * size : (h + 1) * size, here].astype(jnp.float32) * score_scale
+            qa[h * LANE : h * LANE + size, :] = scaled.astype(low_type)
             qa[h * LANE + size : h * LANE + size + 16, :] = apart[:, here]
         acc[...] = jnp.zeros_like(acc)
         low, high = key_range(lengths, first_row + q0, first_row + q0 + BQ - 1)
@@ -226,13 +230,15 @@
                 top, total = carry[2 * h], carry[2 * h + 1]
                 own = slice(h * LANE, (h + 1) * LANE)
                 rows = slice(h * size, (h + 1) * size)
-                s = plain_product(kn[pl.ds(k0, BK), own], qa[own, :]) + bias_part(bias, h, row)
+                s = plain_product(rows_in[pl.ds(k0, BK), own], qa[own, :])
+                s = s + bias_part(bias, h, row)
                 new_top = jnp.maximum(top, jnp.max(s, axis=0, keepdims=True))
                 fade = jnp.exp(top - new_top)
                 p = jnp.exp(s - new_top)
                 total = total * fade + jnp.sum(p, axis=0, keepdims=True)
                 acc[rows, :] = acc[rows, :] * fade + plain_product(
-                    vT[rows, pl.ds(k0, BK)], p.astype(low_type)
+                    cols[2 * width + h * size : 2 * width + (h + 1) * size, pl.ds(k0, BK)],
+                    p.astype(low_type),
                 )
                 out += [new_top, total]
             return tuple(out)
@@ -253,21 +259,17 @@
             ctx_o[pl.ds(at, LANE), :] = turned[b * LANE : (b + 1) * LANE, :]
 
 
-def attention_forward(first_row, lengths, origin, qT, kn, vT, apart, bias):
-    width, rows_here = qT.shape
+def attention_forward(lengths, origin, cols, rows_in, apart, bias):
+    width, rows_here = cols.shape[0] // 3, cols.shape[1]
     heads = bias.shape[0]
-
-    def body(*refs):
-        forward_kernel(first_row, *refs)
-
     return pl.pallas_call(
-        body,
+        forward_kernel,
         out_shape=(
             jax.ShapeDtypeStruct((rows_here, width), low_type),
             jax.ShapeDtypeStruct((width, rows_here), jnp.float32),
             jax.ShapeDtypeStruct((heads, rows_here), jnp.float32),
         ),
-        in_specs=[smem()] * 2 + [vmem()] * 5,
+        in_specs=[smem()] * 2 + [vmem()] * 4,
         out_specs=(vmem(),) * 3,
         scratch_shapes=[
             pltpu.VMEM((heads * LANE, BQ), low_type),
@@ -278,7 +280,7 @@
             flops=rows_here * width, bytes_accessed=width * TOK_DEV, transcendentals=0
         ),
         name="attention_forward",
-    )(lengths, origin, qT, kn, vT, apart, bias)
+    )(lengths, origin, cols, rows_in, apart, bias)
 
 
 def three_parts(values):
@@ -289,10 +291,10 @@
 
 
 def backward_kernel(
-    lengths, origin, qT, kn, vn, kT, dcn, ctxT, lse, apart, bias,
+    lengths, origin, cols, rows_in, dcn, ctxT, lse, apart, bias,
     dT_o, dn_o, lines_o, qa, da, dq, dk, dv, tiles,
 ):
-    width, tokens = qT.shape
+    width, tokens = cols.shape[0] // 3, cols.shape[1]
     heads = bias.shape[0]
     size = width // heads
     for ref in (qa, da, dk, dv, tiles):
@@ -314,7 +316,8 @@
         for h in range(heads):
             rows = slice(h * size, (h + 1) * size)
             top = h * LANE
-            qa[top : top + size, :] = qT[rows, here]
+            scaled = cols[rows, here].astype(jnp.float32) * score_scale
+            qa[top : top + size, :] = scaled.astype(low_type)
             extra = apart[:, here].astype(jnp.float32) + in_depth(-lse[h : h + 1, here])
             qa[top + size : top + size + 16, :] = extra.astype(low_type)
             da[top : top + size, :] = dcT[rows, :].astype(low_type)
@@ -332,9 +335,11 @@
                 rows = slice(h * size, (h + 1) * size)
                 own = slice(h * LANE, (h + 1) * LANE)
                 flat = slice(h * LANE, h * LANE + size)
-                s = plain_product(kn[there, own], qa[own, :])
+                values = slice((heads + h) * LANE, (heads + h + 1) * LANE)
+                keys = slice(width + h * size, width + (h + 1) * size)
+                s = plain_product(rows_in[there, own], qa[own, :])
                 p = jnp.exp(s + bias_part(bias, h, row))
-                ds = p * plain_product(vn[there, own], da[own, :])
+                ds = p * plain_product(rows_in[there, values], da[own, :])
                 for b in range(BQ // LANE):
                     window = pl.ds(pl.multiple_of(row - b * LANE, LANE), BK)
                     tiles[h, window, :] = (
@@ -344,7 +349,7 @@
                 ds_low = ds.astype(low_type)
                 dv[rows, there] = dv[rows, there] + times_transposed(da[flat, :], p_low)
                 dk[rows, there] = dk[rows, there] + times_transposed(qa[flat, :], ds_low)
-                dq[rows, :] = dq[rows, :] + plain_product(kT[rows, there], ds_low)
+                dq[rows, :] = dq[rows, :] + plain_product(cols[keys, there], ds_low)
 
         grad = dq[...] * score_scale
         dT_o[0:width, here] = grad.astype(low_type)
@@ -378,8 +383,8 @@
             lines_o[h, REACH + 1 - d : REACH + 2 - d, :] = jnp.sum(line, axis=0, keepdims=True)
 
 
-def attention_backward(lengths, origin, qT, kn, vn, kT, dcn, ctxT, lse, apart, bias):
-    width, tokens = qT.shape
+def attention_backward(lengths, origin, cols, rows_in, dcn, ctxT, lse, apart, bias):
+    width, tokens = cols.shape[0] // 3, cols.shape[1]
     heads = bias.shape[0]
     return pl.pallas_call(
         backward_kernel,
@@ -388,7 +393,7 @@
             jax.ShapeDtypeStruct((tokens, 3 * width), low_type),
             jax.ShapeDtypeStruct((heads, LINES, LANE), jnp.float32),
         ),
-        in_specs=[smem()] * 2 + [vmem()] * 9,
+        in_specs=[smem()] * 2 + [vmem()] * 7,
         out_specs=(vmem(),) * 3,
         scratch_shapes=[
             pltpu.VMEM((heads * LANE, BQ), low_type),
@@ -403,7 +408,7 @@
             flops=tokens * width, bytes_accessed=width * TOK_DEV, transcendentals=0
         ),
         name="attention_backward",
-    )(lengths, origin, qT, kn, vn, kT, dcn, ctxT, lse, apart, bias)
+    )(lengths, origin, cols, rows_in, dcn, ctxT, lse, apart, bias)
 
 
 def feed_forward_backward_kernel(
@@ -444,6 +449,28 @@
         cost_estimate=pl.CostEstimate(flops=FF * D, bytes_accessed=FF * D, transcendentals=0),
         name="feed_forward_backward",
     )(grad, rows, hidden, slope, inner, outer)
+
+
+def assemble(places, pieces):
+    group = pieces[0].shape[0]
+
+    def body(places_in, *refs):
+        for s, piece in enumerate(refs[:-1]):
+
+            @pl.when(places_in[pl.program_id(0)] == s)
+            def _(piece=piece):
+                refs[-1][...] = piece[...].astype(jnp.float32)
+
+    return pl.pallas_call(
+        body,
+        grid=(len(pieces),),
+        out_shape=jax.ShapeDtypeStruct((len(pieces) * group, D), jnp.float32),
+        in_specs=[smem()] + [pl.BlockSpec((group, D), lambda g: (0, 0))] * len(pieces),
+        out_specs=pl.BlockSpec((group, D), lambda g: (g, 0)),
+        compiler_params=pltpu.CompilerParams(vmem_limit_bytes=VMEM_LIMIT),
+        cost_estimate=pl.CostEstimate(flops=D, bytes_accessed=group * D, transcendentals=0),
+        name="assemble",
+    )(places, *pieces)
 
 
 def loss_kernel(place, numbers, parts, proj_weight, gain, out_slope, out_low, out_row, out_gain):
@@ -592,11 +619,6 @@
         return swap(rows, narrow, peer)
 
     evens = bits[1:]
-    fetched = [
-        [fetch(rows, peer, in_parts) for peer in evens]
-        for rows, in_parts in zip(crossing, (True, False, True))
-    ]
-
     def exchanged(pieces):
         return [
             [(near_index, rows)]
@@ -641,10 +663,7 @@
 
     all_rows = layer_argument.astype(jnp.float32)
     normed_one = (all_rows * rms_scale(all_rows) * rescaling_coefficients[0]).astype(low_type)
-    transposed_rows = times_transposed(qkv_weight, normed_one)
-    query_cols = (transposed_rows[:unit_rows] * score_scale).astype(low_type)
-    key_cols = transposed_rows[unit_rows : 2 * unit_rows].astype(low_type)
-    value_cols = transposed_rows[2 * unit_rows :].astype(low_type)
+    qkv_turned = times_transposed(qkv_weight, normed_one).astype(low_type)
     spread_weight = jnp.pad(
         qkv_weight[unit_rows:].reshape(2 * heads_here, head_size, D),
         ((0, 0), (0, LANE - head_size), (0, 0)),
@@ -657,16 +676,19 @@
     key_value_rows = (
         times_transposed(normed_one, spread_weight) + marks.astype(jnp.float32)
     ).astype(low_type)
-    key_rows = key_value_rows[:, : heads_here * LANE]
-    value_rows = key_value_rows[:, heads_here * LANE :]
     row_place = jnp.arange(16, dtype=jnp.int32)[:, None]
     apart = jnp.where(
         jnp.logical_and(row_place < SEQS_DEV, row_place != segment_ids[None, :]), masked_score, 0.0
     ).astype(low_type)
+    crossing[1] = after(crossing[1], key_value_rows)
+    fetched = [
+        [fetch(rows, peer, in_parts) for peer in evens]
+        for rows, in_parts in zip(crossing, (True, False, True))
+    ]
     inner_parts = exchanged(fetched[0])
-    query_cols = after(query_cols, fetched[0][0])
+    apart = after(apart, fetched[0][0])
     context, context_cols, log_rows = attention_forward(
-        0, lengths, origin, query_cols, key_rows, value_cols, apart, tiles_bias
+        lengths, origin, qkv_turned, key_value_rows, apart, tiles_bias
     )
 
     flat = [rows for pieces in fetched[1:] for rows in pieces]
@@ -791,10 +813,8 @@
     qkv_cols, qkv_rows, bias_lines = attention_backward(
         lengths,
         origin,
-        query_cols,
-        key_rows,
-        value_rows,
-        key_cols,
+        qkv_turned,
+        key_value_rows,
         context_grad,
         context_cols,
         log_rows,
@@ -813,24 +833,28 @@
     late = jnp.concatenate(
         [plain_product(qkv_cols, normed_one).astype(low_type), out_grad], axis=0
     ).reshape(far_count, near_count, part_rows, D)
+    qkv_rows = after(qkv_rows, late)
     half = qkv_rows.shape[0] // 2
     rows_sent = plain_product(qkv_rows[half:], qkv_weight).astype(low_type)
-    rows_kept = plain_product(qkv_rows[:half], after(qkv_weight, rows_sent))
+    normed_one_grad = plain_product(qkv_rows[:half], after(qkv_weight, rows_sent)) + swap(
+        rows_sent, narrow, bits[0]
+    ).astype(jnp.float32)
+    for bit in bits[1:]:
+        half = normed_one_grad.shape[0] // 2
+        rows_sent = normed_one_grad[half:].astype(low_type)
+        normed_one_grad = normed_one_grad[:half] + swap(rows_sent, narrow, bit).astype(
+            jnp.float32
+        )
     late_sum = lax.dynamic_index_in_dim(late, near_index, 1, keepdims=False)
     for peer in range(1, near_count):
         sent = lax.dynamic_index_in_dim(late, near_index ^ peer, 1, keepdims=False)
-        late_sum = sum_low(late_sum, after(swap(sent, near, peer), rows_kept))
+        late_sum = sum_low(late_sum, after(swap(sent, near, peer), rows_sent))
     early = after(near_part, late).reshape(-1, 2, group_rows // part_rows, part_rows, D)
     early = jnp.swapaxes(early, 1, 2).reshape(far_count, 2, part_rows, D)
     terms = jnp.concatenate([early, late_sum[:, None]], axis=1)
     own_part = lax.psum_scatter(
         terms.reshape(far_count * 3 * part_rows, D), far, scatter_dimension=0, tiled=True
     )
-    normed_one_grad = rows_kept + swap(rows_sent, narrow, bits[0]).astype(jnp.float32)
-    for bit in bits[1:]:
-        half = normed_one_grad.shape[0] // 2
-        came = swap(normed_one_grad[half:].astype(low_type), narrow, bit)
-        normed_one_grad = normed_one_grad[:half] + came.astype(jnp.float32)
     input_norm_grad, attn_gain_grad = norm_backward(
         own_rows, scale_one, rescaling_coefficients[0], normed_one_grad
     )
@@ -849,16 +873,15 @@
         ]
     )
     small_all = spread(small, everyone).reshape(wide_count, narrow_count, 4, D)
-    def gathered(rows, other):
-        for bit in reversed(bits):
-            came = swap(rows, narrow, bit)
-            if bit == bits[-1]:
-                came = after(came, other)
-            rows = jnp.concatenate([rows, came], axis=0)
-        return natural_rows(rows, places).astype(jnp.float32)
-
-    input_grad = gathered(input_own.astype(low_type), small_all)
-    layer_result = gathered(after(result_low, input_own), small_all)
+    def gathered(own):
+        pieces = {0: own, 1: swap(own, narrow, 1)}
+        for peer in evens:
+            rows = after(swap(own, narrow, peer), small_all)
+            pieces[peer], pieces[peer + 1] = rows, swap(rows, narrow, 1)
+        return assemble(jnp.stack(places), [pieces[peer] for peer in order])
+
+    input_grad = gathered(input_own.astype(low_type))
+    layer_result = gathered(after(result_low, input_own))
     gain_sums = jnp.sum(small_all[:, :, :2], axis=(0, 1))
     gain_total = jnp.stack([gain_sums[1], gain_sums[0], final_gain_grad[0]])
     bias_all = jnp.sum(small_all[:, :, 2], axis=0)

time: 491 us -> 485 us (0.988)
  other arithmetic: 60.9 us -> 42.8 us
  waiting for transfers between devices: 145 us -> 161 us
  local copies, waits for them, and re-layouts: 39.3 us -> 30.4 us
  Pallas kernels: 111 us -> 116 us
    pallas_call x1 -> x3, Pallas kernels: 34.3 us -> 42.8 us  [the longest x1 31.6 us: attention_forward(): pl.pallas_call(forward_kernel, out_shape=(jax.ShapeDtypeStruct((rows_here...]
    reduce_scatter x1, waiting for transfers between devices: 0.91 us -> 9.33 us  [on_device(): lax.psum_scatter(terms.reshape(far_count * 3 * part_rows, D), far, scatte...]
    convert_element_type x3 -> x0, other arithmetic: 8.17 us -> none  [the longest x2 6.99 us: gathered(): return natural_rows(rows, places).astype(jnp.float32)]
    ppermute x30 -> x32, waiting for transfers between devices: 98.1 us -> 105 us  [swap(): return lax.ppermute(values, axes, [(i, i ^ bit) for i in range(count)])]
    concatenate x3 -> x0, other arithmetic: 6.09 us -> none  [gathered(): rows = jnp.concatenate([rows, came], axis=0)]
    unnamed x130 -> x131, local copies, waits for them, and re-layouts: 8.17 us -> 10.6 us
    ppermute x30 -> x32, starting transfers between devices: 16.3 us -> 18.1 us  [swap(): return lax.ppermute(values, axes, [(i, i ^ bit) for i in range(count)])]
  transfers between devices with their start and end apart: 36 -> 38, of which waited for: 14 -> 14; matrix products, arithmetic and copies ran while one was open for 25% -> 18% of each run, Pallas kernels for 18% -> 19%
where the time goes in v1:
time: 485 us; the launch traced here: 477 us
  waiting for transfers between devices  161 us (33%)
  Pallas kernels  116 us (24%)
  between operations  59.8 us (12%)
  other arithmetic  42.8 us (9%)
  matrix products  39.3 us (8%)
  local copies, waits for them, and re-layouts  30.4 us (6%)
  starting transfers between devices  27.2 us (6%)
    ppermute x32, waiting for transfers between devices, swap(): return lax.ppermute(values, axes, [(i, i ^ bit) for i in range(count)])  105 us
    pallas_call x1, Pallas kernels, attention_backward(): pl.pallas_call(backward_kernel, out_shape=(jax.ShapeDtypeStruct((3 * widt...  44.6 us
    all_gather x1, waiting for transfers between devices, on_device(): lax.all_gather(precise_parameter_blocks.astype(low_type), wide, axis=0, t...  32.7 us
    pallas_call x1, Pallas kernels, attention_forward(): pl.pallas_call(forward_kernel, out_shape=(jax.ShapeDtypeStruct((rows_here...  31.6 us
    pallas_call x1, Pallas kernels, feed_forward_backward(): pl.pallas_call(feed_forward_backward_kernel, grid=(FF // UNIT_BLOCK,), ou...  19.5 us
    dot_general x4, matrix products, times_transposed(): lax.dot_general(left_side, right_side, (((1,), (1,)), ((), ())), preferre...  19.5 us
    ppermute x32, starting transfers between devices, swap(): return lax.ppermute(values, axes, [(i, i ^ bit) for i in range(count)])  18.1 us
    dot_general x5, matrix products, plain_product(): return jnp.dot(left_side, right_side, preferred_element_type=jnp.float32)  13.8 us
  transfers between devices with their start and end apart: 38, of which 14 were waited for; matrix products, arithmetic and copies ran while one was open for 18% of the time, Pallas kernels for 19%

profile of v1, /device:TPU:0, one launch (start us, length us, event | category | flops | bytes accessed | tf_op | source)
XLA Modules:
  0.0 477.2 jit_solution(3424753712312276792)
XLA Ops:
  7.3 2.1 convert_element_type.134
  29.6 1.9 fusion.53
  35.5 1.6 convolution_bitcast_fusion
  41.8 5.4 %bias_tiles.1.bias = f32[3,4224,128]{2,1,0:T(8,128)} custom-call(f32[3,18,128]{2,1,0:T(8,128)} %reshape.269.chunks), custom_call_target="tpu_custom_call" | custom-call | tf_op jit(solution)/shard_map/bias_tiles/pallas_call | solution.py:175
  57.0 3.0 fusion
  60.7 32.7 %all-gather.3.cloned.1.call-done = bf16[16,192,768]{2,1,0:T(8,128)(2,1)} async-done(((bf16[2,192,768]{2,1,0:T(8,128)(2,1)}), bf16[16,192,768]{2,1,0:T(8,128)(2,1)}) %all-gather.3.cloned.1.call-update) | async-done | bytes 4718608 | tf_op jit(solution)/shard_map/all_gather | solution.py:594
  93.5 2.3 dynamic-slice_bitcast_fusion.1
  96.9 1.6 copy-done.6
  98.5 5.8 %add_convert_fusion.1.rows_in = bf16[2560,768]{1,0:T(8,128)(2,1)} fusion(bf16[768,768]{1,0:T(8,128)(2,1)S(1)} %bitcast.177, s32[768]{0:T(1024)S(1)} %fusion.45, s32[2560]{0:T(1024)S(1)} %convert_reduce_fusion, pred[768]{0:T(1024)(128)(4,1)S(1)} %compare_and_fusion, bf16[2560,768]{1,0:T(8,128)(2,1)S(1)} %copy-done.6, f32[768]{0:T(1024)S(1)} %get-tuple-element.213, ...), kind=kOutput, calls=%fused_computation.9 | convolution fusion | flops 3037593600 | bytes 9071360 | tf_op jit(solution)/shard_map/dot_general | solution.py:41
  104.3 1.5 collective-permute-start
  106.4 1.5 collective-permute-start.2
  108.7 1.9 copy-done.1
  110.7 4.2 convolution_convert_fusion.cols
  114.9 5.7 %collective-permute-done = bf16[1,384,768]{2,1,0:T(8,128)(2,1)} collective-permute-done((bf16[1,384,768]{2,1,0:T(8,128)(2,1)S(1)}, bf16[1,384,768]{2,1,0:T(8,128)(2,1)}, u32[]{:S(2)}, u32[]{:S(2)}) %collective-permute-start) | collective-permute-done | bytes 589856 | tf_op jit(solution)/shard_map/ppermute | solution.py:82
  121.9 31.6 %attention_forward.1 = (bf16[2560,192]{1,0:T(8,128)(2,1)}, f32[192,2560]{1,0:T(8,128)}, f32[3,2560]{1,0:T(4,128)}) custom-call(s32[4]{0:T(128)} %bitcast.181, s32[20]{0:T(128)} %fusion.51.origin, bf16[576,2560]{1,0:T(8,128)(2,1)} %convolution_convert_fusion.cols, bf16[2560,768]{1,0:T(8,128)(2,1)} %add_convert_fusion.1.rows_in, ...), custom_call_target="tpu_custom_call" | custom-call | flops 491520 | bytes 491520 | tf_op jit(solution)/shard_map/attention_forward/pallas_call | solution.py:265
  153.5 2.5 bitcast_dynamic-update-slice_fusion
  156.0 1.5 bitcast_dynamic-update-slice_fusion.2
  158.1 1.3 collective-permute-start.6
  160.3 1.3 bitcast_dynamic-update-slice_fusion.7
  163.4 4.5 collective-permute-done.6
  168.4 6.8 %collective-permute-done.4 = bf16[640,192]{1,0:T(8,128)(2,1)S(1)} collective-permute-done((bf16[640,192]{1,0:T(8,128)(2,1)S(1)}, bf16[640,192]{1,0:T(8,128)(2,1)S(1)}, u32[]{:S(2)}, u32[]{:S(2)}) %collective-permute-start.4) | collective-permute-done | bytes 245792 | tf_op jit(solution)/shard_map/ppermute | solution.py:82
  175.2 2.5 multiply_reduce_fusion.4
  178.0 1.6 collective-permute-start.16
  179.6 1.1 bitcast_dynamic-update-slice_fusion.9
  180.8 8.6 %add_convert_fusion = (bf16[640,3072]{1,0:T(8,128)(2,1)}, bf16[640,3072]{1,0:T(8,128)(2,1)S(1)}) fusion(bf16[640,768]{1,0:T(8,128)(2,1)S(1)} %multiply_convert_fusion.1.rows, bf16[3072,768]{1,0:T(8,128)(2,1)S(1)} %bitcast.156), kind=kOutput, calls=%fused_computation.5 | convolution fusion | flops 3057254400 | bytes 13565952 | tf_op jit(solution)/shard_map/dot_general | solution.py:41
  191.6 3.3 multiply_reduce_fusion.3
  197.3 5.0 %all-to-all-start = ((f32[32,4,768]{2,1,0:T(4,128)}), f32[32,4,768]{2,1,0:T(4,128)S(1)}, u32[]{:S(2)}, u32[]{:S(2)}) async-start(f32[32,4,768]{2,1,0:T(4,128)} %broadcast_in_dim.137), calls=%async_computation | async-start | bytes 786432 | tf_op jit(solution)/shard_map/all_to_all | solution.py:136
  202.4 1.2 pad_add_fusion.place
  203.8 1.1 pad_maximum_fusion.4.proj_weight
  204.9 10.5 %all-to-all-done = f32[32,4,768]{2,1,0:T(4,128)S(1)} async-done(((f32[32,4,768]{2,1,0:T(4,128)}), f32[32,4,768]{2,1,0:T(4,128)S(1)}, u32[]{:S(2)}, u32[]{:S(2)}) %all-to-all-start) | async-done | bytes 393248 | tf_op jit(solution)/shard_map/all_to_all | solution.py:136
  216.4 3.9 contrastive.1
  221.8 2.1 fusion.19.grad
  223.9 19.5 %feed_forward_backward.1 = (bf16[32,2,96,768]{3,2,1,0:T(8,128)(2,1)}, f32[640,768]{1,0:T(8,128)}) custom-call(bf16[640,768]{1,0:T(8,128)(2,1)} %fusion.19.grad, bf16[640,768]{1,0:T(8,128)(2,1)} %copy-done.14, bf16[640,3072]{1,0:T(8,128)(2,1)} %copy-done.12, bf16[640,3072]{1,0:T(8,128)(2,1)} %get-tuple-element.227.slope, bf16[3072,768]{1,0:T(8,128)(2,1)} %bitcast.157, ...), custom_call_target="tpu_custom_call" | custom-call | flops 2359296 | bytes 2359296 | tf_op jit(solution)/shard_map/feed_forward_backward/pallas_call | solution.py:439
  243.5 2.8 multiply_reduce_fusion
  246.8 2.6 fusion.65
  251.4 1.4 convolution_convert_fusion.2
  254.4 1.1 collective-permute-start.18
  256.6 6.1 %collective-permute-done.20 = bf16[640,192]{1,0:T(8,128)(2,1)S(1)} collective-permute-done((bf16[640,192]{1,0:T(8,128)(2,1)S(1)}, bf16[640,192]{1,0:T(8,128)(2,1)S(1)}, u32[]{:S(2)}, u32[]{:S(2)}) %collective-permute-start.20) | collective-permute-done | bytes 245792 | tf_op jit(solution)/shard_map/ppermute | solution.py:82
  262.7 9.0 %collective-permute-done.18 = bf16[640,192]{1,0:T(8,128)(2,1)S(1)} collective-permute-done((bf16[640,192]{1,0:T(8,128)(2,1)S(1)}, bf16[640,192]{1,0:T(8,128)(2,1)S(1)}, u32[]{:S(2)}, u32[]{:S(2)}) %collective-permute-start.18) | collective-permute-done | bytes 245792 | tf_op jit(solution)/shard_map/ppermute | solution.py:82
  271.7 1.3 pad_maximum_fusion.1.dcn
  273.0 44.6 %attention_backward.1 = (bf16[576,2560]{1,0:T(8,128)(2,1)}, bf16[2560,576]{1,0:T(8,128)(2,1)}, f32[3,18,128]{2,1,0:T(8,128)}) custom-call(s32[4]{0:T(128)} %bitcast.183, s32[20]{0:T(128)} %fusion.51.origin, bf16[576,2560]{1,0:T(8,128)(2,1)} %convolution_convert_fusion.cols, bf16[2560,768]{1,0:T(8,128)(2,1)} %add_convert_fusion.1.rows_in, ...), custom_call_target="tpu_custom_call" | custom-call | flops 491520 | bytes 491520 | tf_op jit(solution)/shard_map/attention_backward/pallas_call | solution.py:389
  317.7 4.6 convolution_convert_fusion.4
  322.4 1.1 copy-done.17
  323.5 1.7 convolution_convert_fusion.1
  325.4 3.8 collective-permute-done.23
  329.2 1.7 convert_add_fusion
  331.0 1.9 copy-done.10
  333.0 8.2 %collective-permute-done.26 = bf16[4,96,768]{2,1,0:T(8,128)(2,1)S(1)} collective-permute-done((bf16[4,96,768]{2,1,0:T(8,128)(2,1)S(1)}, bf16[4,96,768]{2,1,0:T(8,128)(2,1)S(1)}, u32[]{:S(2)}, u32[]{:S(2)}) %collective-permute-start.26) | collective-permute-done | bytes 589856 | tf_op jit(solution)/shard_map/ppermute | solution.py:82
  341.3 2.6 pad_maximum_fusion
  344.7 1.5 fusion.3
  346.2 21.2 %collective-permute-done.24 = bf16[640,768]{1,0:T(8,128)(2,1)S(1)} collective-permute-done((bf16[640,768]{1,0:T(8,128)(2,1)S(1)}, bf16[640,768]{1,0:T(8,128)(2,1)S(1)}, u32[]{:S(2)}, u32[]{:S(2)}) %collective-permute-start.24) | collective-permute-done | bytes 983072 | tf_op jit(solution)/shard_map/ppermute | solution.py:82
  367.4 2.7 fusion.11
  370.2 2.6 fusion.8.refs_0_
  372.8 9.3 %reduce-scatter.5.cloned.1.call-done = bf16[288,768]{1,0:T(8,128)(2,1)} async-done(((bf16[1152,768]{1,0:T(8,128)(2,1)}), bf16[288,768]{1,0:T(8,128)(2,1)}) %reduce-scatter.5.cloned.1.call-update) | async-done | bytes 442384 | tf_op jit(solution)/shard_map/reduce_scatter | solution.py:855
  383.9 1.1 fusion.27
  385.2 1.6 collective-permute-start.29
  389.7 4.0 all-to-all-start.1
  394.2 39.4 %collective-permute-done.25.refs_1_ = bf16[640,768]{1,0:T(8,128)(2,1)} collective-permute-done((bf16[640,768]{1,0:T(8,128)(2,1)S(1)}, bf16[640,768]{1,0:T(8,128)(2,1)}, u32[]{:S(2)}, u32[]{:S(2)}) %collective-permute-start.25) | collective-permute-done | bytes 983072 | tf_op jit(solution)/shard_map/ppermute | solution.py:82
  435.5 3.1 pad_add_fusion.1.places_in
  442.3 5.6 %assemble.2 = f32[2560,768]{1,0:T(8,128)} custom-call(s32[4]{0:T(128)} %pad_add_fusion.1.places_in, bf16[640,768]{1,0:T(8,128)(2,1)} %copy-done.15, bf16[640,768]{1,0:T(8,128)(2,1)} %collective-permute-done.25.refs_1_, bf16[640,768]{1,0:T(8,128)(2,1)} %collective-permute-done.27.refs_2_, bf16[640,768]{1,0:T(8,128)(2,1)} %collective-permute-done.28.refs_3_), custom_call_target="tpu_custom_call" | custom-call | flops 768 | bytes 491520 | tf_op jit(solution)/shard_map/assemble/pallas_call | solution.py:464
  448.0 5.6 %assemble.3 = f32[2560,768]{1,0:T(8,128)} custom-call(s32[4]{0:T(128)} %pad_add_fusion.1.places_in, bf16[640,768]{1,0:T(8,128)(2,1)} %copy-done.13, bf16[640,768]{1,0:T(8,128)(2,1)} %collective-permute-done.29.refs_1_, bf16[640,768]{1,0:T(8,128)(2,1)} %collective-permute-done.30.refs_2_, bf16[640,768]{1,0:T(8,128)(2,1)} %collective-permute-done.31.refs_3_), custom_call_target="tpu_custom_call" | custom-call | flops 768 | bytes 491520 | tf_op jit(solution)/shard_map/assemble/pallas_call | solution.py:464
  453.7 3.5 all-gather.5.cloned.1.call-done
  461.9 1.1 constant_dynamic-slice_fusion.1
  463.2 2.5 multiply_subtract_fusion.1
  (276 shorter events, 36.9 us)
Async XLA Ops:
  7.2 27.1 %copy-start.45 = (s32[4]{0:T(128)S(1)}, s32[4]{0:T(128)}, u32[]{:S(2)}) copy-start(s32[4]{0:T(128)} %constant.253.clone) | copy-start | bytes 52
  7.2 26.8 %copy-start.46 = (s32[2047]{0:T(1024)S(1)}, s32[2047]{0:T(1024)}, u32[]{:S(2)}) copy-start(s32[2047]{0:T(1024)} %param.19) | copy-start | bytes 24568
  7.2 28.3 %copy-start.49 = (f32[32,3]{0,1:T(4,128)S(1)}, f32[32,3]{0,1:T(4,128)}, u32[]{:S(2)}) copy-start(f32[32,3]{0,1:T(4,128)} %param.27) | copy-start | bytes 1156
  7.2 33.7 %copy-start.47 = (s32[1,4]{1,0:T(1,128)S(1)}, s32[1,4]{1,0:T(1,128)}, u32[]{:S(2)}) copy-start(s32[1,4]{1,0:T(1,128)} %param.18) | copy-start | bytes 52
  7.2 86.2 %all-gather.3.cloned.1.call-start = ((), (), s32[]{:S(2)}) async-start(), calls=%async_computation.4 | async-start | bytes 5308416 | tf_op jit(solution)/shard_map/all_gather | solution.py:594
  41.8 14.6 %copy-start.29 = (f32[3,768]{1,0:T(4,128)S(1)}, f32[3,768]{1,0:T(4,128)}, u32[]{:S(2)}) copy-start(f32[3,768]{1,0:T(4,128)} %param.24) | copy-start | bytes 27652
  57.0 53.7 %copy-start.31 = (f32[768]{0:T(1024)}, f32[768]{0:T(1024)S(1)}, u32[]{:S(2)}) copy-start(f32[768]{0:T(1024)S(1)} %get-tuple-element.213) | copy-start | bytes 9220
  60.0 50.7 %copy-start.38 = (f32[2560]{0:T(1024)}, f32[2560]{0:T(1024)S(1)}, u32[]{:S(2)}) copy-start(f32[2560]{0:T(1024)S(1)} %add_rsqrt_fusion) | copy-start | bytes 30724
  95.9 60.1 %collective-permute-start.9 = (bf16[2,384,768]{2,1,0:T(8,128)(2,1)S(1)}, bf16[2,384,768]{2,1,0:T(8,128)(2,1)}, u32[]{:S(2)}, u32[]{:S(2)}) collective-permute-start(bf16[2,384,768]{2,1,0:T(8,128)(2,1)S(1)} %bitcast.161), channel_id=1, source_target_pairs={{0,1},{1,0},{2,3},{3,2},{4,5},{5,4},{6,7},{7,6},{8,9},{9,8},{10,11... | collective-permute-start | bytes 3538952 | tf_op jit(solution)/shard_map/ppermute | solution.py:82
  96.1 14.7 %copy-start.16 = (bf16[576,768]{1,0:T(8,128)(2,1)}, bf16[576,768]{1,0:T(8,128)(2,1)S(1)}, u32[]{:S(2)}) copy-start(bf16[576,768]{1,0:T(8,128)(2,1)S(1)} %pad_maximum_fusion.7) | copy-start | bytes 2654212
  96.3 57.2 %collective-permute-start.12 = (bf16[2,384,768]{2,1,0:T(8,128)(2,1)S(1)}, bf16[2,384,768]{2,1,0:T(8,128)(2,1)}, u32[]{:S(2)}, u32[]{:S(2)}) collective-permute-start(bf16[2,384,768]{2,1,0:T(8,128)(2,1)S(1)} %bitcast.164), channel_id=1, source_target_pairs={{0,1},{1,0},{2,3},{3,2},{4,5},{5,4},{6,7},{7,6},{8,9},{9,8},{10,11... | collective-permute-start | bytes 3538952 | tf_op jit(solution)/shard_map/ppermute | solution.py:82
  104.3 16.3 %collective-permute-start = (bf16[1,384,768]{2,1,0:T(8,128)(2,1)S(1)}, bf16[1,384,768]{2,1,0:T(8,128)(2,1)}, u32[]{:S(2)}, u32[]{:S(2)}) collective-permute-start(bf16[1,384,768]{2,1,0:T(8,128)(2,1)S(1)} %constant_dynamic-slice_fusion.8), channel_id=1, source_target_pairs={{0,2},{1,3},{2,0},{3,1},{4,6},{5,7},{6,4},{7,5},{8,10},{9,11},{10,... | collective-permute-start | bytes 1769480 | tf_op jit(solution)/shard_map/ppermute | solution.py:82
  105.8 51.7 %collective-permute-start.1 = (bf16[192,768]{1,0:T(8,128)(2,1)S(1)}, bf16[192,768]{1,0:T(8,128)(2,1)}, u32[]{:S(2)}, u32[]{:S(2)}) collective-permute-start(bf16[192,768]{1,0:T(8,128)(2,1)S(1)} %get-tuple-element.77), channel_id=1, source_target_pairs={{0,2},{1,3},{2,0},{3,1},{4,6},{5,7},{6,4},{7,5},{8,10},{9,11},{10,... | collective-permute-start | bytes 884744 | tf_op jit(solution)/shard_map/ppermute | solution.py:82
  106.4 51.1 %collective-permute-start.2 = (bf16[1,384,768]{2,1,0:T(8,128)(2,1)S(1)}, bf16[1,384,768]{2,1,0:T(8,128)(2,1)}, u32[]{:S(2)}, u32[]{:S(2)}) collective-permute-start(bf16[1,384,768]{2,1,0:T(8,128)(2,1)S(1)} %constant_dynamic-slice_fusion.7), channel_id=1, source_target_pairs={{0,2},{1,3},{2,0},{3,1},{4,6},{5,7},{6,4},{7,5},{8,10},{9,11},{10,... | collective-permute-start | bytes 1769480 | tf_op jit(solution)/shard_map/ppermute | solution.py:82
  120.6 37.0 %collective-permute-start.3 = (bf16[1,384,768]{2,1,0:T(8,128)(2,1)}, bf16[1,384,768]{2,1,0:T(8,128)(2,1)}, u32[]{:S(2)}, u32[]{:S(2)}) collective-permute-start(bf16[1,384,768]{2,1,0:T(8,128)(2,1)} %collective-permute-done), channel_id=1, source_target_pairs={{0,4},{4,0},{1,5},{5,1},{2,6},{6,2},{3,7},{7,3},{8,12},{12,8},{9,1... | collective-permute-start | bytes 1769480 | tf_op jit(solution)/shard_map/ppermute | solution.py:82
  153.5 9.2 %collective-permute-start.7 = (bf16[192,768]{1,0:T(8,128)(2,1)S(1)}, bf16[192,768]{1,0:T(8,128)(2,1)S(1)}, u32[]{:S(2)}, u32[]{:S(2)}) collective-permute-start(bf16[192,768]{1,0:T(8,128)(2,1)S(1)} %get-tuple-element.77), channel_id=1, source_target_pairs={{0,1},{1,0},{2,3},{3,2},{4,5},{5,4},{6,7},{7,6},{8,9},{9,8},{10,11... | collective-permute-start | bytes 884744 | tf_op jit(solution)/shard_map/ppermute | solution.py:82
  157.6 5.2 %collective-permute-start.8 = (bf16[192,768]{1,0:T(8,128)(2,1)}, bf16[192,768]{1,0:T(8,128)(2,1)S(1)}, u32[]{:S(2)}, u32[]{:S(2)}) collective-permute-start(bf16[192,768]{1,0:T(8,128)(2,1)} %collective-permute-done.1), channel_id=1, source_target_pairs={{0,1},{1,0},{2,3},{3,2},{4,5},{5,4},{6,7},{7,6},{8,9},{9,8},{10,11... | collective-permute-start | bytes 884744 | tf_op jit(solution)/shard_map/ppermute | solution.py:82
  158.1 17.1 %copy-start.22 = (bf16[640,192]{1,0:T(8,128)(2,1)}, bf16[640,192]{1,0:T(8,128)(2,1)S(1)}, u32[]{:S(2)}) copy-start(bf16[640,192]{1,0:T(8,128)(2,1)S(1)} %get-tuple-element.245) | copy-start | bytes 737284
  158.1 9.8 %collective-permute-start.6 = (bf16[640,192]{1,0:T(8,128)(2,1)S(1)}, bf16[640,192]{1,0:T(8,128)(2,1)S(1)}, u32[]{:S(2)}, u32[]{:S(2)}) collective-permute-start(bf16[640,192]{1,0:T(8,128)(2,1)S(1)} %get-tuple-element.246), channel_id=1, source_target_pairs={{0,3},{1,2},{2,1},{3,0},{4,7},{5,6},{6,5},{7,4},{8,11},{9,10},{10,... | collective-permute-start | bytes 737288 | tf_op jit(solution)/shard_map/ppermute | solution.py:82
  159.4 8.5 %collective-permute-start.5 = (bf16[640,192]{1,0:T(8,128)(2,1)S(1)}, bf16[640,192]{1,0:T(8,128)(2,1)S(1)}, u32[]{:S(2)}, u32[]{:S(2)}) collective-permute-start(bf16[640,192]{1,0:T(8,128)(2,1)S(1)} %get-tuple-element.247), channel_id=1, source_target_pairs={{0,1},{1,0},{2,3},{3,2},{4,5},{5,4},{6,7},{7,6},{8,9},{9,8},{10,11... | collective-permute-start | bytes 737288 | tf_op jit(solution)/shard_map/ppermute | solution.py:82
  159.8 15.4 %collective-permute-start.4 = (bf16[640,192]{1,0:T(8,128)(2,1)S(1)}, bf16[640,192]{1,0:T(8,128)(2,1)S(1)}, u32[]{:S(2)}, u32[]{:S(2)}) collective-permute-start(bf16[640,192]{1,0:T(8,128)(2,1)S(1)} %get-tuple-element.248), channel_id=1, source_target_pairs={{0,2},{1,3},{2,0},{3,1},{4,6},{5,7},{6,4},{7,5},{8,10},{9,11},{10,... | collective-permute-start | bytes 737288 | tf_op jit(solution)/shard_map/ppermute | solution.py:82
  162.7 16.9 %collective-permute-start.10 = (bf16[1,384,768]{2,1,0:T(8,128)(2,1)}, bf16[1,384,768]{2,1,0:T(8,128)(2,1)S(1)}, u32[]{:S(2)}, u32[]{:S(2)}) collective-permute-start(bf16[1,384,768]{2,1,0:T(8,128)(2,1)} %collective-permute-done), channel_id=1, source_target_pairs={{0,1},{1,0},{2,3},{3,2},{4,5},{5,4},{6,7},{7,6},{8,9},{9,8},{10,11... | collective-permute-start | bytes 1769480 | tf_op jit(solution)/shard_map/ppermute | solution.py:82
  162.8 28.3 %collective-permute-start.13 = (bf16[1,384,768]{2,1,0:T(8,128)(2,1)}, bf16[1,384,768]{2,1,0:T(8,128)(2,1)S(1)}, u32[]{:S(2)}, u32[]{:S(2)}) collective-permute-start(bf16[1,384,768]{2,1,0:T(8,128)(2,1)} %collective-permute-done.2), channel_id=1, source_target_pairs={{0,1},{1,0},{2,3},{3,2},{4,5},{5,4},{6,7},{7,6},{8,9},{9,8},{10,11... | collective-permute-start | bytes 1769480 | tf_op jit(solution)/shard_map/ppermute | solution.py:82
  163.4 14.3 %copy-start.27 = (bf16[768,768]{1,0:T(8,128)(2,1)}, bf16[768,768]{1,0:T(8,128)(2,1)S(1)}, u32[]{:S(2)}) copy-start(bf16[768,768]{1,0:T(8,128)(2,1)S(1)} %constant_dynamic-update-slice_fusion) | copy-start | bytes 3538948
  167.9 21.5 %collective-permute-start.14 = (bf16[1,384,768]{2,1,0:T(8,128)(2,1)}, bf16[1,384,768]{2,1,0:T(8,128)(2,1)S(1)}, u32[]{:S(2)}, u32[]{:S(2)}) collective-permute-start(bf16[1,384,768]{2,1,0:T(8,128)(2,1)} %collective-permute-done.2), channel_id=1, source_target_pairs={{0,4},{4,0},{1,5},{5,1},{2,6},{6,2},{3,7},{7,3},{8,12},{12,8},{9,1... | collective-permute-start | bytes 1769480 | tf_op jit(solution)/shard_map/ppermute | solution.py:82
  167.9 12.8 %collective-permute-start.11 = (bf16[1,384,768]{2,1,0:T(8,128)(2,1)}, bf16[1,384,768]{2,1,0:T(8,128)(2,1)S(1)}, u32[]{:S(2)}, u32[]{:S(2)}) collective-permute-start(bf16[1,384,768]{2,1,0:T(8,128)(2,1)} %collective-permute-done.3), channel_id=1, source_target_pairs={{0,1},{1,0},{2,3},{3,2},{4,5},{5,4},{6,7},{7,6},{8,9},{9,8},{10,11... | collective-permute-start | bytes 1769480 | tf_op jit(solution)/shard_map/ppermute | solution.py:82
  177.7 13.8 %copy-start.4 = (f32[640,768]{1,0:T(8,128)}, f32[640,768]{1,0:T(8,128)S(1)}, u32[]{:S(2)}) copy-start(f32[640,768]{1,0:T(8,128)S(1)} %get-tuple-element.287) | copy-start | bytes 5898244
  178.0 11.4 %collective-permute-start.16 = (bf16[192,768]{1,0:T(8,128)(2,1)S(1)}, bf16[192,768]{1,0:T(8,128)(2,1)S(1)}, u32[]{:S(2)}, u32[]{:S(2)}) collective-permute-start(bf16[192,768]{1,0:T(8,128)(2,1)S(1)} %get-tuple-element.83), channel_id=1, source_target_pairs={{0,2},{1,3},{2,0},{3,1},{4,6},{5,7},{6,4},{7,5},{8,10},{9,11},{10,... | collective-permute-start | bytes 884744 | tf_op jit(solution)/shard_map/ppermute | solution.py:82
  189.4 2.1 collective-permute-start.15
  190.6 13.1 %collective-permute-start.17 = (bf16[384,768]{1,0:T(8,128)(2,1)}, bf16[384,768]{1,0:T(8,128)(2,1)S(1)}, u32[]{:S(2)}, u32[]{:S(2)}) collective-permute-start(bf16[384,768]{1,0:T(8,128)(2,1)} %pad_maximum_fusion.8), channel_id=1, source_target_pairs={{0,1},{1,0},{2,3},{3,2},{4,5},{5,4},{6,7},{7,6},{8,9},{9,8},{10,11... | collective-permute-start | bytes 1769480 | tf_op jit(solution)/shard_map/ppermute | solution.py:82
  197.3 18.2 %all-to-all-start = ((f32[32,4,768]{2,1,0:T(4,128)}), f32[32,4,768]{2,1,0:T(4,128)S(1)}, u32[]{:S(2)}, u32[]{:S(2)}) async-start(f32[32,4,768]{2,1,0:T(4,128)} %broadcast_in_dim.137), calls=%async_computation | async-start | bytes 786432 | tf_op jit(solution)/shard_map/all_to_all | solution.py:136
  202.3 139.0 %reduce-scatter.3.cloned.1.call-start = ((), (), s32[]{:S(2)}) async-start(), calls=%async_computation.5 | async-start | bytes 10616832 | tf_op jit(solution)/shard_map/reduce_scatter | solution.py:790
  203.8 17.4 %copy-start.35 = (pred[640]{0:T(1024)(128)(4,1)S(1)}, pred[640]{0:T(1024)(128)(4,1)}, u32[]{:S(2)}) copy-start(pred[640]{0:T(1024)(128)(4,1)} %get-tuple-element.262) | copy-start | bytes 1924
  203.8 17.4 %copy-start.36 = (pred[640]{0:T(1024)(128)(4,1)S(1)}, pred[640]{0:T(1024)(128)(4,1)}, u32[]{:S(2)}) copy-start(pred[640]{0:T(1024)(128)(4,1)} %get-tuple-element.263) | copy-start | bytes 1924
  203.8 17.4 %copy-start.37 = (pred[640]{0:T(1024)(128)(4,1)S(1)}, pred[640]{0:T(1024)(128)(4,1)}, u32[]{:S(2)}) copy-start(pred[640]{0:T(1024)(128)(4,1)} %get-tuple-element.264) | copy-start | bytes 1924
  243.5 138.7 %reduce-scatter.5.cloned.1.call-start = ((), (), s32[]{:S(2)}) async-start(), calls=%async_computation.6 | async-start | bytes 2211840 | tf_op jit(solution)/shard_map/reduce_scatter | solution.py:855
  249.5 144.2 %copy-start.15 = (bf16[640,768]{1,0:T(8,128)(2,1)}, bf16[640,768]{1,0:T(8,128)(2,1)S(1)}, u32[]{:S(2)}) copy-start(bf16[640,768]{1,0:T(8,128)(2,1)S(1)} %get-tuple-element.104.refs_0_) | copy-start | bytes 2949124
  252.9 2.6 collective-permute-start.21
  253.3 9.5 %collective-permute-start.20 = (bf16[640,192]{1,0:T(8,128)(2,1)S(1)}, bf16[640,192]{1,0:T(8,128)(2,1)S(1)}, u32[]{:S(2)}, u32[]{:S(2)}) collective-permute-start(bf16[640,192]{1,0:T(8,128)(2,1)S(1)} %get-tuple-element.254), channel_id=1, source_target_pairs={{0,3},{1,2},{2,1},{3,0},{4,7},{5,6},{6,5},{7,4},{8,11},{9,10},{10,... | collective-permute-start | bytes 737288 | tf_op jit(solution)/shard_map/ppermute | solution.py:82
  253.9 8.8 %collective-permute-start.19 = (bf16[640,192]{1,0:T(8,128)(2,1)S(1)}, bf16[640,192]{1,0:T(8,128)(2,1)S(1)}, u32[]{:S(2)}, u32[]{:S(2)}) collective-permute-start(bf16[640,192]{1,0:T(8,128)(2,1)S(1)} %get-tuple-element.255), channel_id=1, source_target_pairs={{0,1},{1,0},{2,3},{3,2},{4,5},{5,4},{6,7},{7,6},{8,9},{9,8},{10,11... | collective-permute-start | bytes 737288 | tf_op jit(solution)/shard_map/ppermute | solution.py:82
  254.4 17.3 %collective-permute-start.18 = (bf16[640,192]{1,0:T(8,128)(2,1)S(1)}, bf16[640,192]{1,0:T(8,128)(2,1)S(1)}, u32[]{:S(2)}, u32[]{:S(2)}) collective-permute-start(bf16[640,192]{1,0:T(8,128)(2,1)S(1)} %get-tuple-element.256), channel_id=1, source_target_pairs={{0,2},{1,3},{2,0},{3,1},{4,6},{5,7},{6,4},{7,5},{8,10},{9,11},{10,... | collective-permute-start | bytes 737288 | tf_op jit(solution)/shard_map/ppermute | solution.py:82
  255.7 61.9 %collective-permute-start.22 = (bf16[192,768]{1,0:T(8,128)(2,1)S(1)}, bf16[192,768]{1,0:T(8,128)(2,1)S(1)}, u32[]{:S(2)}, u32[]{:S(2)}) collective-permute-start(bf16[192,768]{1,0:T(8,128)(2,1)S(1)} %slice.216), channel_id=1, source_target_pairs={{0,2},{1,3},{2,0},{3,1},{4,6},{5,7},{6,4},{7,5},{8,10},{9,11},{10,... | collective-permute-start | bytes 884744 | tf_op jit(solution)/shard_map/ppermute | solution.py:82
  273.0 44.7 %copy-start.7 = (bf16[2560,768]{1,0:T(8,128)(2,1)S(1)}, bf16[2560,768]{1,0:T(8,128)(2,1)}, u32[]{:S(2)}) copy-start(bf16[2560,768]{1,0:T(8,128)(2,1)} %param.17) | copy-start | bytes 11796484
  273.0 44.7 %copy-start.32 = (f32[768]{0:T(1024)S(1)}, f32[768]{0:T(1024)}, u32[]{:S(2)}) copy-start(f32[768]{0:T(1024)} %copy-done.31) | copy-start | bytes 9220
  273.0 44.7 %copy-start.39 = (f32[2560]{0:T(1024)S(1)}, f32[2560]{0:T(1024)}, u32[]{:S(2)}) copy-start(f32[2560]{0:T(1024)} %copy-done.38) | copy-start | bytes 30724
  325.2 4.0 collective-permute-start.23
  325.3 15.8 %collective-permute-start.26 = (bf16[4,96,768]{2,1,0:T(8,128)(2,1)S(1)}, bf16[4,96,768]{2,1,0:T(8,128)(2,1)S(1)}, u32[]{:S(2)}, u32[]{:S(2)}) collective-permute-start(bf16[4,96,768]{2,1,0:T(8,128)(2,1)S(1)} %dynamic-slice_bitcast_fusion), channel_id=1, source_target_pairs={{0,4},{4,0},{1,5},{5,1},{2,6},{6,2},{3,7},{7,3},{8,12},{12,8},{9,1... | collective-permute-start | bytes 1769480 | tf_op jit(solution)/shard_map/ppermute | solution.py:82
  344.0 113.2 %all-gather.5.cloned.1.call-start = ((), (), s32[]{:S(2)}) async-start(), calls=%async_computation.7 | async-start | bytes 3981312 | tf_op jit(solution)/shard_map/all_gather | solution.py:862
  344.0 23.4 %collective-permute-start.24 = (bf16[640,768]{1,0:T(8,128)(2,1)S(1)}, bf16[640,768]{1,0:T(8,128)(2,1)S(1)}, u32[]{:S(2)}, u32[]{:S(2)}) collective-permute-start(bf16[640,768]{1,0:T(8,128)(2,1)S(1)} %slice.252), channel_id=1, source_target_pairs={{0,2},{1,3},{2,0},{3,1},{4,6},{5,7},{6,4},{7,5},{8,10},{9,11},{10,... | collective-permute-start | bytes 2949128 | tf_op jit(solution)/shard_map/ppermute | solution.py:82
  346.2 23.9 %copy-start.8 = (f32[640,768]{1,0:T(8,128)S(1)}, f32[640,768]{1,0:T(8,128)}, u32[]{:S(2)}) copy-start(f32[640,768]{1,0:T(8,128)} %get-tuple-element.226) | copy-start | bytes 5898244
  370.2 13.7 %copy-start.41 = (s32[2304]{0:T(1024)S(1)}, s32[2304]{0:T(1024)}, u32[]{:S(2)}) copy-start(s32[2304]{0:T(1024)} %copy-done.40) | copy-start | bytes 27652
  370.2 13.7 %copy-start.61 = (f32[3,18,128]{2,1,0:T(8,128)S(1)}, f32[3,18,128]{2,1,0:T(8,128)}, u32[]{:S(2)}) copy-start(f32[3,18,128]{2,1,0:T(8,128)} %get-tuple-element.105) | copy-start | bytes 82948
  372.8 75.1 %copy-start.13 = (bf16[640,768]{1,0:T(8,128)(2,1)}, bf16[640,768]{1,0:T(8,128)(2,1)S(1)}, u32[]{:S(2)}) copy-start(bf16[640,768]{1,0:T(8,128)(2,1)S(1)} %fusion.8.refs_0_) | copy-start | bytes 2949124
  372.8 65.8 %copy-start.48 = (f32[1,128]{1,0:T(1,128)S(1)}, f32[1,128]{1,0:T(1,128)}, u32[]{:S(2)}) copy-start(f32[1,128]{1,0:T(1,128)} %get-tuple-element.90) | copy-start | bytes 1540
  372.8 68.2 %copy-start.44 = (f32[1,768]{1,0:T(1,128)S(1)}, f32[1,768]{1,0:T(1,128)}, u32[]{:S(2)}) copy-start(f32[1,768]{1,0:T(1,128)} %get-tuple-element.114) | copy-start | bytes 9220
  385.2 48.9 %collective-permute-start.29 = (bf16[640,768]{1,0:T(8,128)(2,1)S(1)}, bf16[640,768]{1,0:T(8,128)(2,1)}, u32[]{:S(2)}, u32[]{:S(2)}) collective-permute-start(bf16[640,768]{1,0:T(8,128)(2,1)S(1)} %fusion.8.refs_0_), channel_id=1, source_target_pairs={{0,2},{1,3},{2,0},{3,1},{4,6},{5,7},{6,4},{7,5},{8,10},{9,11},{10,... | collective-permute-start | bytes 2949128 | tf_op jit(solution)/shard_map/ppermute | solution.py:82
  386.7 47.0 %collective-permute-start.25 = (bf16[640,768]{1,0:T(8,128)(2,1)S(1)}, bf16[640,768]{1,0:T(8,128)(2,1)}, u32[]{:S(2)}, u32[]{:S(2)}) collective-permute-start(bf16[640,768]{1,0:T(8,128)(2,1)S(1)} %get-tuple-element.104.refs_0_), channel_id=1, source_target_pairs={{0,2},{1,3},{2,0},{3,1},{4,6},{5,7},{6,4},{7,5},{8,10},{9,11},{10,... | collective-permute-start | bytes 2949128 | tf_op jit(solution)/shard_map/ppermute | solution.py:82
  389.7 44.0 %all-to-all-start.1 = ((f32[32,4,768]{2,1,0:T(4,128)}), f32[32,4,768]{2,1,0:T(4,128)S(1)}, u32[]{:S(2)}, u32[]{:S(2)}) async-start(f32[32,4,768]{2,1,0:T(4,128)} %broadcast_in_dim.146), calls=%async_computation.3 | async-start | bytes 786432 | tf_op jit(solution)/shard_map/all_to_all | solution.py:136
  393.7 48.6 %collective-permute-start.27 = (bf16[640,768]{1,0:T(8,128)(2,1)S(1)}, bf16[640,768]{1,0:T(8,128)(2,1)}, u32[]{:S(2)}, u32[]{:S(2)}) collective-permute-start(bf16[640,768]{1,0:T(8,128)(2,1)S(1)} %get-tuple-element.104.refs_0_), channel_id=1, source_target_pairs={{0,1},{1,0},{2,3},{3,2},{4,5},{5,4},{6,7},{7,6},{8,9},{9,8},{10,11... | collective-permute-start | bytes 2949128 | tf_op jit(solution)/shard_map/ppermute | solution.py:82
  394.1 53.9 %collective-permute-start.30 = (bf16[640,768]{1,0:T(8,128)(2,1)S(1)}, bf16[640,768]{1,0:T(8,128)(2,1)}, u32[]{:S(2)}, u32[]{:S(2)}) collective-permute-start(bf16[640,768]{1,0:T(8,128)(2,1)S(1)} %fusion.8.refs_0_), channel_id=1, source_target_pairs={{0,1},{1,0},{2,3},{3,2},{4,5},{5,4},{6,7},{7,6},{8,9},{9,8},{10,11... | collective-permute-start | bytes 2949128 | tf_op jit(solution)/shard_map/ppermute | solution.py:82
  433.7 8.6 %collective-permute-start.28 = (bf16[640,768]{1,0:T(8,128)(2,1)}, bf16[640,768]{1,0:T(8,128)(2,1)}, u32[]{:S(2)}, u32[]{:S(2)}) collective-permute-start(bf16[640,768]{1,0:T(8,128)(2,1)} %collective-permute-done.25.refs_1_), channel_id=1, source_target_pairs={{0,1},{1,0},{2,3},{3,2},{4,5},{5,4},{6,7},{7,6},{8,9},{9,8},{10,11... | collective-permute-start | bytes 2949128 | tf_op jit(solution)/shard_map/ppermute | solution.py:82
  434.1 13.9 %collective-permute-start.31 = (bf16[640,768]{1,0:T(8,128)(2,1)}, bf16[640,768]{1,0:T(8,128)(2,1)}, u32[]{:S(2)}, u32[]{:S(2)}) collective-permute-start(bf16[640,768]{1,0:T(8,128)(2,1)} %collective-permute-done.29.refs_1_), channel_id=1, source_target_pairs={{0,1},{1,0},{2,3},{3,2},{4,5},{5,4},{6,7},{7,6},{8,9},{9,8},{10,11... | collective-permute-start | bytes 2949128 | tf_op jit(solution)/shard_map/ppermute | solution.py:82
  448.0 13.3 %copy-start.50 = (f32[32,3]{0,1:T(4,128)S(1)}, f32[32,3]{0,1:T(4,128)}, u32[]{:S(2)}) copy-start(f32[32,3]{0,1:T(4,128)} %param.27) | copy-start | bytes 1156
  448.0 13.3 %copy-start.51 = (f32[32,3]{0,1:T(4,128)S(1)}, f32[32,3]{0,1:T(4,128)}, u32[]{:S(2)}) copy-start(f32[32,3]{0,1:T(4,128)} %param.29) | copy-start | bytes 1156
  (36 other events, 204.7 us)
Sparse Core Ops, SparseCore 0:
  10.8 82.5 all-gather.2
  243.6 79.5 reduce-scatter.2
  344.1 38.0 reduce-scatter.4
  384.4 72.6 all-gather.4
